TPU v7x, 256 devices: a whole 4x4x8 slice. The times are simulated.
256 devices in a mesh: ctx: 64 (over y_lo, x, z), tp: 4 (over y_hi, core).
Axes of the slice: x: 4, y: 4 (y_hi: 2, y_lo: 2; y = y_hi * 2 + y_lo), z: 8, core: 2. Of those that a mesh axis runs over, the one named last changes fastest.
Arguments:
- q_pre: bfloat16 [2, 4096, 4096], P(None, 'ctx', 'tp'), may hold values from -8 to 8
- k_pre: bfloat16 [2, 4096, 512], P(None, 'ctx', 'tp'), may hold values from -8 to 8
- value_before_filter: bfloat16 [2, 4096, 512], P(None, 'ctx', 'tp'), may hold values from -8 to 8
- d_out: bfloat16 [2, 4096, 4096], P(None, 'ctx', 'tp'), may hold values from -8 to 8
- filters: float32 [3, 3, 128], replicated, may hold values from 0.5 to 1.5
- doc_lengths: int32 [8], replicated, may hold values from 1 to 4096, 8192 in all
Outputs:
- d_q_pre: float32 [2, 4096, 4096], P(None, 'ctx', 'tp')
- d_k_pre: float32 [2, 4096, 512], P(None, 'ctx', 'tp')
- d_v_pre: float32 [2, 4096, 512], P(None, 'ctx', 'tp')
- d_filters: float32 [3, 3, 128], replicated
Inputs may be any that keep to these rules, and one draw needn't show every extreme that they name: `doc_lengths`: the lengths sum to 8192, and the longest document has exactly 4096 positions.
All inputs are finite; a program needn't handle non-finite values.
Results may differ from a plain program's by a relative error of at most 0.009.
The roundings to bfloat16 on the way count: a program that leaves them out, or rounds other values in their place, can miss the bound.
Values may be sent and summed in bfloat16 or wider, within the bound.
A program may use at most 128 MiB of HBM per device.

v0:
```python
import jax
import jax.numpy as jnp
from jax import lax
from jax.sharding import PartitionSpec as P


def padded(block, sides, width):
    for axis, dim in sides:
        count = lax.axis_size(axis)
        forward = [(i, i + 1) for i in range(count - 1)]
        backward = [(target, source) for source, target in forward]
        low = lax.ppermute(
            lax.slice_in_dim(block, block.shape[dim] - width, None, axis=dim), axis, forward
        )
        high = lax.ppermute(lax.slice_in_dim(block, 0, width, axis=dim), axis, backward)
        block = jnp.concatenate([low, block, high], axis=dim)
    return block


def doc_index(places, starts):
    return jnp.sum((places[..., None] >= starts).astype(jnp.int32), axis=-1) - 1


def shards(q_pre, k_pre, value_before_filter, d_out, filters, doc_lengths):
    ctx_count = lax.axis_size("ctx")
    ctx_index = lax.axis_index("ctx")
    span_rows = q_pre.shape[1]
    half_rows = span_rows * ctx_count
    head_size = filters.shape[2]
    tap_count = filters.shape[1]
    query_head_rows = q_pre.shape[2] // head_size
    shared_heads = k_pre.shape[2] // head_size
    group_size = query_head_rows // shared_heads
    score_scale = head_size ** (-0.5)
    starts = jnp.cumsum(doc_lengths) - doc_lengths
    offsets = jnp.arange(span_rows, dtype=jnp.int32)
    own_places = jnp.stack(
        [ctx_index * span_rows + offsets, (2 * ctx_count - 1 - ctx_index) * span_rows + offsets]
    )
    own_docs = doc_index(own_places, starts)
    is_middle = ctx_index == ctx_count - 1
    edge_one = q_pre.shape[2]
    edge_two = edge_one + k_pre.shape[2]
    edge_three = edge_two + value_before_filter.shape[2]
    back_docs = [
        doc_index(own_places - tap_index, starts) == own_docs for tap_index in range(tap_count)
    ]
    ahead_docs = [
        doc_index(own_places + tap_index, starts) == own_docs for tap_index in range(tap_count)
    ]
    early_tail = jnp.concatenate(
        [q_pre[0, -2:], k_pre[0, -2:], value_before_filter[0, -2:]], axis=1
    )
    late_tail = jnp.concatenate([q_pre[1, -2:], k_pre[1, -2:], value_before_filter[1, -2:]], axis=1)
    input_rims = padded(jnp.concatenate([late_tail, early_tail], axis=0), (("ctx", 0),), 2)
    before_early = input_rims[0:2]
    before_late = jnp.where(is_middle, early_tail, input_rims[6:8])

    def extend_input(source, lower_edge, upper_edge):
        early_rows = jnp.concatenate([before_early[:, lower_edge:upper_edge], source[0]], axis=0)
        late_rows = jnp.concatenate([before_late[:, lower_edge:upper_edge], source[1]], axis=0)
        return jnp.stack([early_rows, late_rows])

    extended = [
        extend_input(q_pre, 0, edge_one),
        extend_input(k_pre, edge_one, edge_two),
        extend_input(value_before_filter, edge_two, edge_three),
    ]

    def convolve(ext_rows, weights):
        head_count = ext_rows.shape[2] // head_size
        grid_rows = ext_rows.astype(jnp.float32).reshape(2, span_rows + 2, head_count, head_size)
        summed = jnp.zeros((2, span_rows, head_count, head_size), jnp.float32)
        for tap_index in range(tap_count):
            window = grid_rows[:, 2 - tap_index : 2 - tap_index + span_rows]
            summed = summed + jnp.where(
                back_docs[tap_index][:, :, None, None], weights[tap_index] * window, 0.0
            )
        return summed.astype(jnp.bfloat16)

    q_conv = convolve(extended[0], filters[0]).reshape(
        2 * span_rows, shared_heads, group_size, head_size
    )
    k_conv = convolve(extended[1], filters[1]).reshape(2, span_rows, shared_heads * head_size)
    v_conv = convolve(extended[2], filters[2]).reshape(2, span_rows, shared_heads * head_size)
    grad_flat = d_out.reshape(2 * span_rows, shared_heads, group_size, head_size)
    query_places = own_places.reshape(-1)
    query_docs = own_docs.reshape(-1)

    def piece_places(start, count):
        rows_at = start + jnp.arange(count, dtype=jnp.int32)
        late_places = (2 * ctx_count - 1 - rows_at // span_rows) * span_rows + rows_at % span_rows
        return (rows_at, late_places)

    def make_allowed(key_places, row_lower):
        key_docs = doc_index(key_places, starts)
        return (query_docs[row_lower:, None] == key_docs[None, :]) & (
            key_places[None, :] <= query_places[row_lower:, None]
        )

    def products(keys_part, values_part, row_lower):
        scores = (
            jnp.einsum(
                "qkgd,nkd->kgqn", q_conv[row_lower:], keys_part, preferred_element_type=jnp.float32
            )
            * score_scale
        )
        prob_grads = jnp.einsum(
            "qkgd,nkd->kgqn", grad_flat[row_lower:], values_part, preferred_element_type=jnp.float32
        )
        return (scores, prob_grads)

    def stats_tile(carry, keys_part, values_part, key_places, row_lower):
        allowed = make_allowed(key_places, row_lower)
        row_max, exp_sums, weighted = carry
        scores, prob_grads = products(keys_part, values_part, row_lower)
        old_max = row_max[..., row_lower:]
        new_max = jnp.maximum(old_max, jnp.max(jnp.where(allowed, scores, -1e30), axis=-1))
        factor = jnp.exp(old_max - new_max)
        exp_terms = jnp.where(allowed, jnp.exp(scores - new_max[..., None]), 0.0)
        row_max = row_max.at[..., row_lower:].set(new_max)
        exp_sums = exp_sums.at[..., row_lower:].set(
            exp_sums[..., row_lower:] * factor + jnp.sum(exp_terms, axis=-1)
        )
        weighted = weighted.at[..., row_lower:].set(
            weighted[..., row_lower:] * factor + jnp.sum(exp_terms * prob_grads, axis=-1)
        )
        return (row_max, exp_sums, weighted)

    def stats_fold(carry, pieces, start):
        key_piece, value_piece = pieces
        count = key_piece.shape[1]
        early_places, late_places = piece_places(start, count)
        key_block = key_piece.reshape(2, count, shared_heads, head_size)
        value_block = value_piece.reshape(2, count, shared_heads, head_size)
        carry = stats_tile(carry, key_block[0], value_block[0], early_places, 0)
        return stats_tile(carry, key_block[1], value_block[1], late_places, span_rows)

    def grads_tile(
        carry,
        keys_part,
        values_part,
        key_places,
        row_lower,
        part_index,
        start,
        log_totals,
        row_sums,
    ):
        allowed = make_allowed(key_places, row_lower)
        query_grads, key_value_grads = carry
        scores, prob_grads = products(keys_part, values_part, row_lower)
        probabilities = jnp.where(allowed, jnp.exp(scores - log_totals[..., row_lower:, None]), 0.0)
        probs_low = probabilities.astype(jnp.bfloat16)
        score_grads = (
            probabilities * (prob_grads - row_sums[..., row_lower:, None]) * score_scale
        ).astype(jnp.bfloat16)
        value_grads = jnp.einsum(
            "kgqn,qkgd->nkd", probs_low, grad_flat[row_lower:], preferred_element_type=jnp.float32
        )
        key_grads = jnp.einsum(
            "kgqn,qkgd->nkd", score_grads, q_conv[row_lower:], preferred_element_type=jnp.float32
        )
        query_grads = query_grads.at[row_lower:].add(
            jnp.einsum("kgqn,nkd->qkgd", score_grads, keys_part, preferred_element_type=jnp.float32)
        )
        count = keys_part.shape[0]
        joined = jnp.concatenate(
            [key_grads.reshape(count, -1), value_grads.reshape(count, -1)], axis=1
        )[None]
        current = lax.dynamic_slice(
            key_value_grads, (part_index, start, 0), (1, count, joined.shape[2])
        )
        key_value_grads = lax.dynamic_update_slice(
            key_value_grads, current + joined, (part_index, start, 0)
        )
        return (query_grads, key_value_grads)

    def make_grads_fold(log_totals, row_sums):

        def grads_fold(carry, pieces, start):
            key_piece, value_piece = pieces
            count = key_piece.shape[1]
            early_places, late_places = piece_places(start, count)
            key_block = key_piece.reshape(2, count, shared_heads, head_size)
            value_block = value_piece.reshape(2, count, shared_heads, head_size)
            carry = grads_tile(
                carry, key_block[0], value_block[0], early_places, 0, 0, start, log_totals, row_sums
            )
            return grads_tile(
                carry,
                key_block[1],
                value_block[1],
                late_places,
                span_rows,
                1,
                start,
                log_totals,
                row_sums,
            )

        return grads_fold

    stats_init = (
        jnp.full((shared_heads, group_size, 2 * span_rows), -1e30, jnp.float32),
        jnp.zeros((shared_heads, group_size, 2 * span_rows), jnp.float32),
        jnp.zeros((shared_heads, group_size, 2 * span_rows), jnp.float32),
    )
    grads_init = (
        jnp.zeros((2 * span_rows, shared_heads, group_size, head_size), jnp.float32),
        jnp.zeros((2, half_rows, 2 * shared_heads * head_size), jnp.float32),
    )
    key_whole, value_whole = (
        lax.all_gather(k_conv, "ctx", axis=1, tiled=True),
        lax.all_gather(v_conv, "ctx", axis=1, tiled=True),
    )
    block_rows = span_rows * min(ctx_count, 8)

    def run_local(fold_fn, init):

        def step_fn(block_index, carry):
            first_row = block_index * block_rows
            pieces = (
                lax.dynamic_slice_in_dim(key_whole, first_row, block_rows, 1),
                lax.dynamic_slice_in_dim(value_whole, first_row, block_rows, 1),
            )
            return fold_fn(carry, pieces, first_row)

        return lax.fori_loop(0, half_rows // block_rows, step_fn, init)

    row_max, exp_sums, weighted = run_local(stats_fold, stats_init)
    log_totals = row_max + jnp.log(exp_sums)
    row_sums = weighted / exp_sums
    query_grads, key_value_grads = run_local(make_grads_fold(log_totals, row_sums), grads_init)
    key_value_share = lax.psum_scatter(key_value_grads, "ctx", scatter_dimension=1, tiled=True)
    query_share = query_grads.reshape(2, span_rows, edge_one)
    grads_all = jnp.concatenate([query_share, key_value_share], axis=2)
    early_head = grads_all[0, :2]
    late_head = grads_all[1, :2]
    grad_rims = padded(jnp.concatenate([early_head, late_head], axis=0), (("ctx", 0),), 2)
    after_late = grad_rims[0:2]
    after_early = jnp.where(is_middle, late_head, grad_rims[6:8])
    grads_ext = jnp.stack(
        [
            jnp.concatenate([grads_all[0], after_early], axis=0),
            jnp.concatenate([grads_all[1], after_late], axis=0),
        ]
    )

    def input_grads(grad_rows, weights):
        head_count = grad_rows.shape[2] // head_size
        grid_rows = grad_rows.reshape(2, span_rows + 2, head_count, head_size)
        summed = jnp.zeros((2, span_rows, head_count, head_size), jnp.float32)
        for tap_index in range(tap_count):
            window = grid_rows[:, tap_index : tap_index + span_rows]
            summed = summed + jnp.where(
                ahead_docs[tap_index][:, :, None, None], weights[tap_index] * window, 0.0
            )
        return summed.reshape(2, span_rows, head_count * head_size)

    def filter_terms(grad_rows, ext_rows):
        head_count = grad_rows.shape[2] // head_size
        grid_grads = grad_rows.reshape(2, span_rows, head_count, head_size)
        grid_inputs = ext_rows.astype(jnp.float32).reshape(2, span_rows + 2, head_count, head_size)
        per_tap = []
        for tap_index in range(tap_count):
            window = grid_inputs[:, 2 - tap_index : 2 - tap_index + span_rows]
            per_tap.append(
                jnp.sum(
                    jnp.where(back_docs[tap_index][:, :, None, None], grid_grads * window, 0.0),
                    axis=(0, 1, 2),
                )
            )
        return jnp.stack(per_tap)

    d_q_pre = input_grads(grads_ext[:, :, 0:edge_one], filters[0])
    d_k_pre = input_grads(grads_ext[:, :, edge_one:edge_two], filters[1])
    d_v_pre = input_grads(grads_ext[:, :, edge_two:edge_three], filters[2])
    local_filters = jnp.stack(
        [
            filter_terms(grads_all[:, :, 0:edge_one], extended[0]),
            filter_terms(grads_all[:, :, edge_one:edge_two], extended[1]),
            filter_terms(grads_all[:, :, edge_two:edge_three], extended[2]),
        ]
    )
    d_filters = lax.psum(local_filters, ("ctx", "tp"))
    return (d_q_pre, d_k_pre, d_v_pre, d_filters)


def solution(mesh):
    return jax.shard_map(
        shards,
        mesh=mesh,
        in_specs=(
            P(None, "ctx", "tp"),
            P(None, "ctx", "tp"),
            P(None, "ctx", "tp"),
            P(None, "ctx", "tp"),
            P(),
            P(),
        ),
        out_specs=(P(None, "ctx", "tp"), P(None, "ctx", "tp"), P(None, "ctx", "tp"), P()),
        check_vma=False,
    )
```

profile of v0, /device:TPU:32, one launch (start us, length us, event | category | flops | bytes accessed | tf_op | source)
XLA Modules:
  0.0 1240.9 jit_solution(4390555037323255116)
XLA Ops:
  9.4 3.8 collective-permute-start.1
  17.2 2.1 collective-permute-start
  19.3 3.4 collective-permute-done
  26.6 300.3 %all-gather.7.cloned.1.call-done = bf16[2,4096,1,128]{3,1,0,2:T(8,128)(2,1)} async-done(((bf16[2,64,1,128]{3,1,0,2:T(8,128)(2,1)}), bf16[2,4096,1,128]{3,1,0,2:T(8,128)(2,1)}) %all-gather.7.cloned.1.call-update) | async-done | bytes 2097168 | tf_op jit(solution)/shard_map/all_gather | solution.py:215
  326.9 299.6 %all-gather.5.cloned.1.call-done = bf16[2,4096,1,128]{3,1,0,2:T(8,128)(2,1)} async-done(((bf16[2,64,1,128]{3,1,0,2:T(8,128)(2,1)}), bf16[2,4096,1,128]{3,1,0,2:T(8,128)(2,1)}) %all-gather.5.cloned.1.call-update) | async-done | bytes 2097168 | tf_op jit(solution)/shard_map/all_gather | solution.py:214
  626.5 62.9 %while.84 = (s32[]{:T(128)}, f32[1,8,128]{2,1,0:T(8,128)S(1)}, f32[1,8,128]{2,1,0:T(8,128)S(1)}, f32[1,8,128]{2,1,0:T(8,128)S(1)}, s32[2,64]{1,0:T(2,128)}, /*in...) while((s32[]{:T(128)}, f32[1,8,128]{2,1,0:T(8,128)S(1)}, ...), condition=%wide.wide.region_13.14_spmd, body=%wide.wide.region_4.13_spmd.sunk | while | flops 411904000 | bytes 11297599 | solution.py:229
  689.4 4.3 broadcast_in_dim.399
  693.7 114.2 %while.85 = (s32[]{:T(128)}, f32[128,1,8,128]{3,0,2,1:T(8,128)S(1)}, f32[2,4096,256]{1,2,0:T(8,128)}, bf16[2,4096,128]{2,1,0:T(8,128)(2,1)}, s32[2,64]{1,0:T(2,1...) while((s32[]{:T(128)}, ...), condition=%wide.wide.region_17.18_spmd, body=%wide.wide.region_14.17_spmd.sunk | while | flops 1013976576 | bytes 22534984 | solution.py:229
  704.1 2.0 fusion.195
  718.4 2.0 fusion.195
  720.3 2.0 fusion.196
  732.7 2.0 fusion.195
  746.9 2.0 fusion.195
  763.1 2.0 fusion.196
  775.4 2.0 fusion.195
  777.4 2.0 fusion.196
  789.7 2.0 fusion.195
  791.7 2.0 fusion.196
  805.9 2.0 fusion.196
  807.9 8.9 copy.62
  817.7 325.4 %reduce-scatter.2.cloned.1.call-done = f32[2,64,256]{2,1,0:T(8,128)} async-done(((f32[2,4096,256]{2,1,0:T(8,128)}), f32[2,64,256]{2,1,0:T(8,128)}) %reduce-scatter.2.cloned.1.call-update) | async-done | bytes 131088 | tf_op jit(solution)/shard_map/reduce_scatter | solution.py:235
  1144.1 2.4 collective-permute-start.3
  1146.6 5.5 collective-permute-start.2
  1153.1 78.9 %psum.7 = f32[3,3,128]{2,1,0:T(4,128)} all-reduce(f32[3,3,128]{2,1,0:T(4,128)S(1)} %pad_maximum_fusion.1), channel_id=1, replica_groups=mesh['ctx'=64,'tp'=4] {'ctx','tp'}, use_global_device_ids=true, to_apply=%region_30.31 | all-reduce | flops 1152 | bytes 9216 | tf_op jit(solution)/shard_map/psum | solution.py:286
  (415 shorter events, 169.0 us)
Async XLA Ops:
  7.2 18.7 %copy-start = (bf16[2,64,1024]{2,1,0:T(8,128)(2,1)S(1)}, bf16[2,64,1024]{2,1,0:T(8,128)(2,1)}, u32[]{:S(2)}) copy-start(bf16[2,64,1024]{2,1,0:T(8,128)(2,1)} %param.34) | copy-start | bytes 786436
  7.2 319.7 %all-gather.7.cloned.1.call-start = ((), (), s32[]{:S(2)}) async-start(), calls=%async_computation.3 | async-start | bytes 2129920 | tf_op jit(solution)/shard_map/all_gather | solution.py:215
  9.4 7.7 collective-permute-start.1
  16.2 10.4 copy-start.1
  17.2 5.5 collective-permute-start
  23.6 603.0 %all-gather.5.cloned.1.call-start = ((), (), s32[]{:S(2)}) async-start(), calls=%async_computation.2 | async-start | bytes 2129920 | tf_op jit(solution)/shard_map/all_gather | solution.py:214
  24.3 1118.8 %reduce-scatter.2.cloned.1.call-start = ((), (), s32[]{:S(2)}) async-start(), calls=%async_computation.1 | async-start | bytes 8519680 | tf_op jit(solution)/shard_map/reduce_scatter | solution.py:235
  24.6 2.0 copy-start.2
  1144.1 87.9 %collective-permute-start.3 = (f32[2,1280]{1,0:T(2,128)S(1)}, f32[2,1280]{1,0:T(2,128)S(1)}, u32[]{:S(2)}, u32[]{:S(2)}) collective-permute-start(f32[2,1280]{1,0:T(2,128)S(1)} %get-tuple-element.1157), channel_id=1, source_target_pairs={{0,4},{4,8},{8,12},{12,16},{16,20},{20,24},{24,28},{28,32},{32,36}... | collective-permute-start | bytes 30728 | tf_op jit(solution)/shard_map/ppermute | solution.py:12
  1146.6 85.4 %collective-permute-start.2 = (f32[2,1280]{1,0:T(2,128)S(1)}, f32[2,1280]{1,0:T(2,128)S(1)}, u32[]{:S(2)}, u32[]{:S(2)}) collective-permute-start(f32[2,1280]{1,0:T(2,128)S(1)} %get-tuple-element.1158), channel_id=1, source_target_pairs={{4,0},{8,4},{12,8},{16,12},{20,16},{24,20},{28,24},{32,28},{36,32}... | collective-permute-start | bytes 30728 | tf_op jit(solution)/shard_map/ppermute | solution.py:15
Sparse Core Ops, SparseCore 0:
  23.7 303.1 all-gather.6
  329.3 297.2 all-gather.4
  816.9 326.1 reduce-scatter.1
where the time goes:
time: 1240 us
  waiting for transfers between devices  929 us (75%)
  matrix products  121 us (10%)
  blocking collectives  78.9 us (6%)
  other arithmetic  51.5 us (4%)
  local copies, waits for them, and re-layouts  30.2 us (2%)
  between operations  14.1 us (1%)
  starting transfers between devices  13.9 us (1%)
    reduce_scatter x1, waiting for transfers between devices, shards(): lax.psum_scatter(key_value_grads, 'ctx', scatter_dimension=1, tiled=True)  325 us
    all_gather x1, waiting for transfers between devices, shards(): lax.all_gather(v_conv, 'ctx', axis=1, tiled=True)  300 us
    all_gather x1, waiting for transfers between devices, shards(): lax.all_gather(k_conv, 'ctx', axis=1, tiled=True)  300 us
    psum x1, blocking collectives, shards(): d_filters = lax.psum(local_filters, ('ctx', 'tp'))  78.9 us
    dot_general x32, matrix products, products(): jnp.einsum('qkgd,nkd->kgqn', grad_flat[row_lower:], values_part, preferre...  43.7 us
    dot_general x32, matrix products, products(): jnp.einsum('qkgd,nkd->kgqn', q_conv[row_lower:], keys_part, preferred_ele...  43.3 us
    dynamic_update_slice x16, other arithmetic, grads_tile(): lax.dynamic_update_slice(key_value_grads, current + joined, (part_index,...  31.3 us
  transfers between devices with their start and end apart: 7, of which 4 were waited for; matrix products, arithmetic and copies ran while one was open for 1% of the time, Pallas kernels for 0%

commit v1 on v0

v1 whole, which is shorter than its diff:
```python
import functools
import math

import jax
import jax.numpy as jnp
from jax import lax
from jax.experimental import pallas as pl
from jax.experimental.pallas import tpu as pltpu
from jax.sharding import PartitionSpec as P

MESH = pl.DeviceIdType.MESH
Y, X, Z = 0, 1, 2
SIZES = (2, 4, 8)
CTX = 64
TP = 4
ROWS = 64
LENGTH = 8192
HEADS = 8
WIDTH = 128
COLS = HEADS * ROWS
TILE = 256
N_TILES = LENGTH // TILE
MAX_TILES = 18
SCALE = WIDTH ** (-0.5)
LOG2E = math.log2(math.e)
F32 = jnp.float32
BF16 = jnp.bfloat16

PLAN = (
    (0, 0, 0, 32, (Y, X, Z)),
    (1, 0, 0, 32, (Y, Z, X)),
    (0, 1, 0, 32, (Z, X, Y)),
    (1, 1, 0, 32, (Y, Z, X)),
    (0, 0, 32, 32, (Y, X, Z)),
    (1, 0, 32, 32, (X, Z, Y)),
    (0, 1, 32, 32, (Y, Z, X)),
    (1, 1, 32, 32, (Z, X, Y)),
)
SLOTS = 13


def gather_hops(n):
    if n == 2:
        return [[(1, 0, None)]]
    if n == 4:
        return [[(1, 0, None), (-1, 0, None)], [(1, -1, 0), (-1, 1, 1)]]
    return [
        [(1, 0, None), (-1, 0, None)],
        [(1, -1, None), (-1, 1, None)],
        [(1, -2, None), (-1, 2, None)],
        [(1, -3, 0), (-1, 3, 1)],
    ]


def coords():
    c = lax.axis_index("ctx")
    return [c // 32, (c // 8) % 4, c % 8]


def ctx_of(co):
    return co[0] * 32 + co[1] * 8 + co[2]


def shifted(co, dim, by):
    co = list(co)
    co[dim] = (co[dim] + by + SIZES[dim]) % SIZES[dim]
    return co


def block_at(half, dim, at):
    return at if half == 0 else SIZES[dim] - 1 - at


def gather_kernel(k_ref, v_ref, q_ref, g_ref, rim_ref, send_sem, recv_sem, rim_send, rim_recv):
    c = lax.axis_index("ctx")
    co = coords()
    after, before = (c + 1) % CTX, (c + CTX - 1) % CTX
    neighbours = [ctx_of(shifted(co, Y, 1)), after, before]
    for dim in (X, Z):
        neighbours += [ctx_of(shifted(co, dim, 1)), ctx_of(shifted(co, dim, -1))]
    barrier = pltpu.get_barrier_semaphore()
    for neighbour in neighbours:
        pl.semaphore_signal(barrier, inc=1, device_id={"ctx": neighbour}, device_id_type=MESH)
    for half in range(2):
        at = [block_at(half, d, co[d]) for d in range(3)]
        g_ref[0, half, at[0], at[1], at[2]] = k_ref[half]
        g_ref[1, half, at[0], at[1], at[2]] = v_ref[half]
    pl.semaphore_wait(barrier, len(neighbours))

    rims = []
    for half, target in ((0, after), (1, before)):
        copy = pltpu.make_async_remote_copy(
            src_ref=q_ref.at[half, pl.ds(ROWS - 16, 16)],
            dst_ref=rim_ref.at[half],
            send_sem=rim_send.at[half],
            recv_sem=rim_recv.at[half],
            device_id={"ctx": target},
            device_id_type=MESH,
        )
        copy.start()
        rims.append(copy)

    def start(chunk, slot, stage, direction, offset, part):
        which, half, row, rows, order = PLAN[chunk]
        dim = order[stage]
        at = [None] * 3
        for s, d in enumerate(order):
            if s < stage:
                at[d] = pl.ds(0, SIZES[d])
            else:
                at[d] = block_at(half, d, shifted(co, d, offset if s == stage else 0)[d])
        if part is not None:
            rows = rows // 2
            row = row + part * rows
        ref = g_ref.at[which, half, at[0], at[1], at[2], pl.ds(row, rows)]
        copy = pltpu.make_async_remote_copy(
            src_ref=ref,
            dst_ref=ref,
            send_sem=send_sem.at[chunk, slot],
            recv_sem=recv_sem.at[chunk, slot],
            device_id={"ctx": ctx_of(shifted(co, dim, direction))},
            device_id_type=MESH,
        )
        copy.start()
        return copy

    hops = []
    for plan in PLAN:
        steps, slot = [], 0
        for stage, dim in enumerate(plan[4]):
            for at, hop in enumerate(gather_hops(SIZES[dim])):
                steps.append((at == 0, [(slot + i, stage) + entry for i, entry in enumerate(hop)]))
                slot += len(hop)
        hops.append(steps)
    copies, flying = [], [[] for _ in PLAN]
    for hop in range(len(hops[0])):
        for chunk in range(len(PLAN)):
            first, entries = hops[chunk][hop]
            if first:
                for copy in flying[chunk]:
                    copy.wait_recv()
            started = []
            for i, entry in enumerate(entries):
                if not first:
                    flying[chunk][i].wait_recv()
                started.append(start(chunk, *entry))
            flying[chunk] = started
            copies += started
    for chunk in range(len(PLAN)):
        for copy in flying[chunk]:
            copy.wait_recv()
    for copy in rims:
        copy.wait()
    for copy in copies:
        copy.wait_send()


def gather(k, v, q):
    return pl.pallas_call(
        gather_kernel,
        out_shape=(
            jax.ShapeDtypeStruct((2, 2) + SIZES + (ROWS, WIDTH), BF16),
            jax.ShapeDtypeStruct((2, 16, HEADS * WIDTH), BF16),
        ),
        in_specs=[pl.BlockSpec(memory_space=pltpu.VMEM)] * 3,
        out_specs=(pl.BlockSpec(memory_space=pltpu.VMEM),) * 2,
        scratch_shapes=[
            pltpu.SemaphoreType.DMA((len(PLAN), SLOTS)),
            pltpu.SemaphoreType.DMA((len(PLAN), SLOTS)),
            pltpu.SemaphoreType.DMA((2,)),
            pltpu.SemaphoreType.DMA((2,)),
        ],
        compiler_params=pltpu.CompilerParams(
            collective_id=1, has_side_effects=True, vmem_limit_bytes=32 << 20
        ),
        name="gather",
    )(k, v, q)


def doc_starts(lengths_ref):
    starts = [jnp.int32(0)]
    for d in range(7):
        starts.append(starts[-1] + lengths_ref[d])
    return starts


def start_of(places, starts):
    found = jnp.zeros_like(places)
    for s in starts[1:]:
        found = jnp.where(places >= s, s, found)
    return found


def attend_kernel(
    lengths_ref, filters_ref, q_ref, rim_ref, do_ref, g_ref,
    dq_ref, out_ref, taps_ref,
    kc_ref, vc_ref, s_ref, dp_ref, dk_ref, dv_ref, qs_ref, dos_ref, dqt_ref,
):
    c = lax.axis_index("ctx")
    starts = doc_starts(lengths_ref)
    ends = (c * ROWS, (2 * CTX - 1 - c) * ROWS)
    first_tiles, last_tiles = [], []
    for half in range(2):
        first_tiles.append(start_of(ends[half], starts) // TILE)
        last_tiles.append((ends[half] + ROWS + TILE - 1) // TILE)

    def clear(tile, _):
        r0 = pl.multiple_of(tile * TILE, TILE)
        dk_ref[pl.ds(r0, TILE)] = jnp.zeros((TILE, WIDTH), F32)
        dv_ref[pl.ds(r0, TILE)] = jnp.zeros((TILE, WIDTH), F32)
        return 0

    lax.fori_loop(0, N_TILES, clear, 0)

    def q_window(half, h):
        lanes = slice(h * WIDTH, (h + 1) * WIDTH)
        before = rim_ref[half, :, lanes]
        if half == 1:
            before = jnp.where(c == CTX - 1, q_ref[0, ROWS - 16 :, lanes], before)
        cat = jnp.concatenate([before.astype(F32), q_ref[half, :, lanes].astype(F32)], axis=0)
        return [cat[16 - s : 16 - s + ROWS] for s in range(3)]

    def q_masks(half):
        places = ends[half] + lax.broadcasted_iota(jnp.int32, (ROWS, WIDTH), 0)
        begin = start_of(places, starts)
        return [places - s >= begin for s in range(1, 3)]

    for half in range(2):
        masks = q_masks(half)
        for h in range(HEADS):
            x = q_window(half, h)
            y = filters_ref[0, 0:1] * x[0]
            for s in range(1, 3):
                y = y + jnp.where(masks[s - 1], filters_ref[0, s : s + 1] * x[s], 0.0)
            qs_ref[half, h * ROWS : (h + 1) * ROWS] = y.astype(BF16)
            dos_ref[half, h * ROWS : (h + 1) * ROWS] = do_ref[half, :, h * WIDTH : (h + 1) * WIDTH]

    def raw_window(which, r0):
        before = g_ref[which, pl.ds(pl.multiple_of(jnp.maximum(r0 - 16, 0), 16), 16)]
        here = g_ref[which, pl.ds(r0, TILE)]
        cat = jnp.concatenate([before.astype(F32), here.astype(F32)], axis=0)
        return [cat[16 - s : 16 - s + TILE] for s in range(3)]

    def tile_masks(r0):
        places = r0 + lax.broadcasted_iota(jnp.int32, (TILE, WIDTH), 0)
        begin = start_of(places, starts)
        return [places - s >= begin for s in range(1, 3)]

    NT = (((1,), (1,)), ((), ()))
    TN = (((0,), (0,)), ((), ()))
    for half in range(2):
        p0 = ends[half]
        t0, t1 = first_tiles[half], last_tiles[half]
        places = p0 + lax.broadcasted_iota(jnp.int32, (1, COLS), 1) % ROWS
        begin = start_of(places, starts)
        last_begin = start_of(p0 + ROWS - 1, starts)

        def stats_step(tile, carry):
            m, l, w = carry
            r0 = pl.multiple_of(tile * TILE, TILE)
            at = pl.multiple_of((tile - t0) * TILE, TILE)
            masks = tile_masks(r0)
            for which, dst in ((0, kc_ref), (1, vc_ref)):
                x = raw_window(which, r0)
                y = filters_ref[1 + which, 0:1] * x[0]
                for s in range(1, 3):
                    y = y + jnp.where(masks[s - 1], filters_ref[1 + which, s : s + 1] * x[s], 0.0)
                dst[pl.ds(r0, TILE)] = y.astype(BF16)
            s_ref[pl.ds(at, TILE)] = (
                lax.dot_general(kc_ref[pl.ds(r0, TILE)], qs_ref[half], NT, preferred_element_type=F32)
                * (SCALE * LOG2E)
            )

            @pl.when(jnp.logical_or(r0 < last_begin, r0 + TILE - 1 > p0))
            def _():
                keys = r0 + lax.broadcasted_iota(jnp.int32, (TILE, COLS), 0)
                allowed = jnp.logical_and(keys <= places, keys >= begin)
                s_ref[pl.ds(at, TILE)] = jnp.where(allowed, s_ref[pl.ds(at, TILE)], -1e30)

            dp_ref[pl.ds(at, TILE)] = (
                lax.dot_general(vc_ref[pl.ds(r0, TILE)], dos_ref[half], NT, preferred_element_type=F32)
                * SCALE
            )
            s = s_ref[pl.ds(at, TILE)].reshape(TILE // 8, 8, COLS)
            dp = dp_ref[pl.ds(at, TILE)].reshape(TILE // 8, 8, COLS)
            m_new = jnp.maximum(m, jnp.max(s, axis=0))
            factor = jnp.exp2(m - m_new)
            p = jnp.exp2(s - m_new[None])
            l = l * factor + jnp.sum(p, axis=0)
            w = w * factor + jnp.sum(p * dp, axis=0)
            return m_new, l, w

        m, l, w = lax.fori_loop(
            t0, t1, stats_step,
            (jnp.full((8, COLS), -1e30, F32), jnp.zeros((8, COLS), F32), jnp.zeros((8, COLS), F32)),
        )
        top = jnp.max(m, axis=0, keepdims=True)
        factor = jnp.exp2(m - top)
        total = jnp.sum(l * factor, axis=0, keepdims=True)
        lse = top + jnp.log2(total)
        mean = jnp.sum(w * factor, axis=0, keepdims=True) / total
        dqt_ref[...] = jnp.zeros((WIDTH, COLS), F32)

        def grads_step(tile, _):
            r0 = pl.multiple_of(tile * TILE, TILE)
            at = pl.multiple_of((tile - t0) * TILE, TILE)
            p = jnp.exp2(s_ref[pl.ds(at, TILE)] - lse)
            ds = (p * (dp_ref[pl.ds(at, TILE)] - mean)).astype(BF16)
            dv_ref[pl.ds(r0, TILE)] += jnp.dot(p.astype(BF16), dos_ref[half], preferred_element_type=F32)
            dk_ref[pl.ds(r0, TILE)] += jnp.dot(ds, qs_ref[half], preferred_element_type=F32)
            dqt_ref[...] += lax.dot_general(kc_ref[pl.ds(r0, TILE)], ds, TN, preferred_element_type=F32)
            return 0

        lax.fori_loop(t0, t1, grads_step, 0)
        dq = jnp.transpose(dqt_ref[...])
        masks = q_masks(half)
        sums = [jnp.zeros((8, WIDTH), F32) for _ in range(3)]
        for h in range(HEADS):
            grad = dq[h * ROWS : (h + 1) * ROWS]
            dq_ref[half, :, h * WIDTH : (h + 1) * WIDTH] = grad
            x = q_window(half, h)
            for s in range(3):
                term = grad * x[s]
                if s:
                    term = jnp.where(masks[s - 1], term, 0.0)
                sums[s] = sums[s] + jnp.sum(term.reshape(ROWS // 8, 8, WIDTH), axis=0)
        if half == 0:
            q_sums = sums
        else:
            q_sums = [a + b for a, b in zip(q_sums, sums)]

    def finish(tile, carry):
        r0 = pl.multiple_of(tile * TILE, TILE)
        inside = jnp.logical_or(
            jnp.logical_and(tile >= first_tiles[0], tile < last_tiles[0]),
            jnp.logical_and(tile >= first_tiles[1], tile < last_tiles[1]),
        )

        def full(carry):
            places = r0 + lax.broadcasted_iota(jnp.int32, (TILE, WIDTH), 0)
            begin = start_of(places, starts)
            masks = [places - s >= begin for s in range(1, 3)]
            ahead = [
                jnp.logical_and(places >= start_of(places + s, starts), places + s < LENGTH)
                for s in range(1, 3)
            ]
            nxt = pl.multiple_of(jnp.minimum(r0 + TILE, LENGTH - 8), 8)
            sums = []
            for which, acc in ((0, dk_ref), (1, dv_ref)):
                x = raw_window(which, r0)
                here = acc[pl.ds(r0, TILE)]
                cat = jnp.concatenate([here, acc[pl.ds(nxt, 8)]], axis=0)
                y = filters_ref[1 + which, 0:1] * here
                for s in range(1, 3):
                    y = y + jnp.where(
                        ahead[s - 1], filters_ref[1 + which, s : s + 1] * cat[s : s + TILE], 0.0
                    )
                out_ref[which, pl.ds(r0, TILE)] = y.astype(BF16)
                for s in range(3):
                    term = here * x[s]
                    if s:
                        term = jnp.where(masks[s - 1], term, 0.0)
                    sums.append(jnp.sum(term.reshape(TILE // 8, 8, WIDTH), axis=0))
            return tuple(a + b for a, b in zip(carry, sums))

        def blank(carry):
            for which in range(2):
                out_ref[which, pl.ds(r0, TILE)] = jnp.zeros((TILE, WIDTH), BF16)
            return carry

        return lax.cond(inside, full, blank, carry)

    sums = lax.fori_loop(0, N_TILES, finish, tuple(jnp.zeros((8, WIDTH), F32) for _ in range(6)))
    sums = list(q_sums) + list(sums)
    taps_ref[...] = jnp.zeros((16, WIDTH), F32)
    for i in range(9):
        taps_ref[i : i + 1] = jnp.sum(sums[i], axis=0, keepdims=True)


def attend(lengths, filters, q, rim, d_out, gathered):
    vmem = pl.BlockSpec(memory_space=pltpu.VMEM)
    return pl.pallas_call(
        attend_kernel,
        out_shape=(
            jax.ShapeDtypeStruct((2, ROWS, HEADS * WIDTH), F32),
            jax.ShapeDtypeStruct((2, LENGTH, WIDTH), BF16),
            jax.ShapeDtypeStruct((16, WIDTH), F32),
        ),
        in_specs=[pl.BlockSpec(memory_space=pltpu.SMEM)] + [vmem] * 5,
        out_specs=(vmem,) * 3,
        scratch_shapes=[
            pltpu.VMEM((LENGTH, WIDTH), BF16),
            pltpu.VMEM((LENGTH, WIDTH), BF16),
            pltpu.VMEM((MAX_TILES * TILE, COLS), F32),
            pltpu.VMEM((MAX_TILES * TILE, COLS), F32),
            pltpu.VMEM((LENGTH, WIDTH), F32),
            pltpu.VMEM((LENGTH, WIDTH), F32),
            pltpu.VMEM((2, COLS, WIDTH), BF16),
            pltpu.VMEM((2, COLS, WIDTH), BF16),
            pltpu.VMEM((WIDTH, COLS), F32),
        ],
        compiler_params=pltpu.CompilerParams(vmem_limit_bytes=56 << 20),
        name="attend",
    )(lengths, filters, q, rim, d_out, gathered)


def reduce_hops(n):
    if n == 2:
        return [[(1, 1, None)]]
    if n == 4:
        return [[(1, 2, None), (-1, -2, None)], [(1, 1, 0), (-1, -1, 1)]]
    return [
        [(1, 4, None), (-1, -4, None)],
        [(1, 3, 0), (-1, -3, 1)],
        [(1, 2, 2), (-1, -2, 2)],
        [(1, 1, 2), (-1, -1, 2)],
    ]


def scatter_kernel(
    lengths_ref, filters_ref, part_ref, dq_ref, taps_ref,
    dqp_ref, dkp_ref, dvp_ref, dfil_ref,
    *scratch,
):
    buffers = scratch[: 3 * len(PLAN)]
    sums = scratch[3 * len(PLAN) : 5 * len(PLAN)]
    rim_ref, tap_z, tap_x, tap_w, send_sem, recv_sem, rim_send, rim_recv, tap_send, tap_recv = scratch[
        5 * len(PLAN) :
    ]
    c = lax.axis_index("ctx")
    tp = lax.axis_index("tp")
    co = coords()
    after, before = (c + 1) % CTX, (c + CTX - 1) % CTX

    me_w = co[Y] * TP + tp
    peers = [
        [(shifted(co, Z, i), tp) for i in range(1, 8)],
        [(shifted(co, X, i), tp) for i in range(1, 4)],
        [],
    ]
    for i in range(1, 8):
        other = (me_w + i) % 8
        peers[2].append(([other // TP, co[X], co[Z]], other % TP))
    barrier = pltpu.get_barrier_semaphore()
    greet = [(ctx_of(place), core) for group in peers for place, core in group] + [(after, tp), (before, tp)]
    for ctx, core in greet:
        pl.semaphore_signal(barrier, inc=1, device_id={"ctx": ctx, "tp": core}, device_id_type=MESH)
    pl.semaphore_wait(barrier, len(greet))

    def send(src, dst, send_at, recv_at, ctx, core):
        copy = pltpu.make_async_remote_copy(
            src_ref=src, dst_ref=dst, send_sem=send_at, recv_sem=recv_at,
            device_id={"ctx": ctx, "tp": core}, device_id_type=MESH,
        )
        copy.start()
        return copy

    all_copies = []

    def start(chunk, hop):
        which, half, row, rows, order = PLAN[chunk]
        stage, entries, at_hop = hops[chunk][hop]
        dims = order[: 3 - stage]
        dim = dims[-1]
        kept = sorted(dims[:-1])
        started = []
        for i, (slot, direction, offset, had) in enumerate(entries):
            target = block_at(half, dim, shifted(co, dim, offset)[dim])

            def own(row_at, count):
                if stage == 0:
                    at = [pl.ds(0, SIZES[d]) for d in range(3)]
                    at[dim] = target
                    return part_ref.at[which, half, at[0], at[1], at[2], pl.ds(row + row_at, count)]
                at = [pl.ds(0, SIZES[d]) if d != dim else target for d in sorted(dims)]
                return sums[2 * chunk + stage - 1].at[(*at, pl.ds(row_at, count))]

            buffer = buffers[3 * chunk + stage]
            whole = tuple(pl.ds(0, SIZES[d]) for d in kept)
            half_rows = rows // 2
            first = at_hop == 0
            n_hops = len(reduce_hops(SIZES[dim]))
            lo, count = (i * half_rows, half_rows) if first and n_hops > 1 else (0, rows)
            if first:
                if stage == 0:
                    src = own(lo, count)
                else:
                    stash = buffer.at[(i, n_hops, *whole, pl.ds(lo, count))]
                    stash[...] = own(lo, count)[...].astype(BF16)
                    src = stash
            else:
                held = buffer.at[(i, at_hop - 1, *whole, pl.ds(0, rows))]
                if had == 2:
                    held[...] = (held[...].astype(F32) + own(0, rows)[...].astype(F32)).astype(BF16)
                else:
                    came = buffer.at[(i, at_hop - 1, *whole, pl.ds(had * half_rows, half_rows))]
                    rest = buffer.at[(i, at_hop - 1, *whole, pl.ds((1 - had) * half_rows, half_rows))]
                    came[...] = (
                        came[...].astype(F32) + own(had * half_rows, half_rows)[...].astype(F32)
                    ).astype(BF16)
                    rest[...] = own((1 - had) * half_rows, half_rows)[...].astype(BF16)
                src = held
            dst = buffer.at[(i, at_hop, *whole, pl.ds(lo, count))]
            started.append(
                send(
                    src, dst, send_sem.at[chunk, slot], recv_sem.at[chunk, slot],
                    ctx_of(shifted(co, dim, direction)), tp,
                )
            )
        all_copies.extend(started)
        return started

    def close_stage(chunk, stage):
        which, half, row, rows, order = PLAN[chunk]
        dims = order[: 3 - stage]
        dim = dims[-1]
        kept = sorted(dims[:-1])
        mine = block_at(half, dim, co[dim])
        buffer = buffers[3 * chunk + stage]
        if stage == 0:
            at = [pl.ds(0, SIZES[d]) for d in range(3)]
            at[dim] = mine
            total = part_ref[which, half, at[0], at[1], at[2], pl.ds(row, rows)].astype(F32)
        else:
            at = [pl.ds(0, SIZES[d]) if d != dim else mine for d in sorted(dims)]
            total = sums[2 * chunk + stage - 1][tuple(at)]
        last = len(reduce_hops(SIZES[dim])) - 1
        whole = tuple(pl.ds(0, SIZES[d]) for d in kept)
        for i in range(1 if SIZES[dim] == 2 else 2):
            total = total + buffer[(i, last, *whole)].astype(F32)
        if stage < 2:
            sums[2 * chunk + stage][...] = total
        else:
            out = dkp_ref if which == 0 else dvp_ref
            out[half, pl.ds(row, rows)] = total

    hops = []
    for plan in PLAN:
        steps, slot = [], 0
        for stage in range(3):
            for at_hop, hop in enumerate(reduce_hops(SIZES[plan[4][2 - stage]])):
                steps.append((stage, [(slot + i,) + entry for i, entry in enumerate(hop)], at_hop))
                slot += len(hop)
        hops.append(steps)

    tap_buffers = (tap_z, tap_x, tap_w)
    tap_me = (co[Z], co[X], me_w)
    tap_copies = []

    def tap_start(stage, value):
        buffer = tap_buffers[stage]
        mine = tap_me[stage]
        buffer[mine] = value
        started = []
        base = sum(len(p) for p in peers[:stage])
        for i, (place, core) in enumerate(peers[stage]):
            started.append(
                send(
                    buffer.at[mine], buffer.at[mine], tap_send.at[base + i], tap_recv.at[base + i],
                    ctx_of(place), core,
                )
            )
        tap_copies.extend(started)
        return started

    def tap_sum(stage, started):
        for copy in started:
            copy.wait_recv()
        buffer = tap_buffers[stage]
        total = buffer[0]
        for i in range(1, buffer.shape[0]):
            total = total + buffer[i]
        return total

    rims = [
        send(dq_ref.at[half, pl.ds(0, 8)], rim_ref.at[half], rim_send.at[half], rim_recv.at[half], target, tp)
        for half, target in ((0, before), (1, after))
    ]
    flying = [start(chunk, 0) for chunk in range(len(PLAN))]
    taps_flying = tap_start(0, taps_ref[...])

    for copy in rims:
        copy.wait_recv()
    starts = doc_starts(lengths_ref)
    for half in range(2):
        p0 = c * ROWS if half == 0 else (2 * CTX - 1 - c) * ROWS
        places = p0 + lax.broadcasted_iota(jnp.int32, (ROWS, WIDTH), 0)
        ahead = [
            jnp.logical_and(places >= start_of(places + s, starts), places + s < LENGTH) for s in range(1, 3)
        ]
        for h in range(HEADS):
            lanes = slice(h * WIDTH, (h + 1) * WIDTH)
            beyond = rim_ref[half, :, lanes]
            if half == 0:
                beyond = jnp.where(c == CTX - 1, dq_ref[1, 0:8, lanes], beyond)
            here = dq_ref[half, :, lanes]
            cat = jnp.concatenate([here, beyond], axis=0)
            y = filters_ref[0, 0:1] * here
            for s in range(1, 3):
                y = y + jnp.where(ahead[s - 1], filters_ref[0, s : s + 1] * cat[s : s + ROWS], 0.0)
            dqp_ref[half, :, lanes] = y

    n_hops = len(hops[0])
    for hop in range(1, n_hops + 1):
        for chunk in range(len(PLAN)):
            for copy in flying[chunk]:
                copy.wait_recv()
            stage = hops[chunk][hop - 1][0]
            if hop == n_hops or hops[chunk][hop][0] != stage:
                close_stage(chunk, stage)
            if hop < n_hops:
                flying[chunk] = start(chunk, hop)
        if hop in (2, 4):
            taps_flying = tap_start(hop // 2, tap_sum(hop // 2 - 1, taps_flying))
    dfil_ref[...] = tap_sum(2, taps_flying)
    for copy in all_copies + tap_copies + rims:
        copy.wait_send()


def scatter(lengths, filters, part, dq, taps):
    vmem = pl.BlockSpec(memory_space=pltpu.VMEM)
    buffers, sums = [], []
    for _, _, _, rows, order in PLAN:
        for stage in range(3):
            dims = order[: 3 - stage]
            kept = tuple(SIZES[d] for d in sorted(dims[:-1]))
            n = SIZES[dims[-1]]
            steps = len(reduce_hops(n)) + (1 if stage else 0)
            buffers.append(pltpu.VMEM((1 if n == 2 else 2, steps) + kept + (rows, WIDTH), BF16))
            if stage < 2:
                sums.append(pltpu.VMEM(kept + (rows, WIDTH), F32))
    return pl.pallas_call(
        scatter_kernel,
        out_shape=(
            jax.ShapeDtypeStruct((2, ROWS, HEADS * WIDTH), F32),
            jax.ShapeDtypeStruct((2, ROWS, WIDTH), F32),
            jax.ShapeDtypeStruct((2, ROWS, WIDTH), F32),
            jax.ShapeDtypeStruct((16, WIDTH), F32),
        ),
        in_specs=[pl.BlockSpec(memory_space=pltpu.SMEM)] + [vmem] * 4,
        out_specs=(vmem,) * 4,
        scratch_shapes=buffers
        + sums
        + [
            pltpu.VMEM((2, 8, HEADS * WIDTH), F32),
            pltpu.VMEM((8, 16, WIDTH), F32),
            pltpu.VMEM((4, 16, WIDTH), F32),
            pltpu.VMEM((8, 16, WIDTH), F32),
            pltpu.SemaphoreType.DMA((len(PLAN), SLOTS)),
            pltpu.SemaphoreType.DMA((len(PLAN), SLOTS)),
            pltpu.SemaphoreType.DMA((2,)),
            pltpu.SemaphoreType.DMA((2,)),
            pltpu.SemaphoreType.DMA((17,)),
            pltpu.SemaphoreType.DMA((17,)),
        ],
        compiler_params=pltpu.CompilerParams(
            collective_id=2, has_side_effects=True, vmem_limit_bytes=40 << 20
        ),
        name="scatter",
    )(lengths, filters, part, dq, taps)


def shards(q_pre, k_pre, value_before_filter, d_out, filters, doc_lengths):
    gathered, rim = gather(k_pre, value_before_filter, q_pre)
    dq, part, taps = attend(
        doc_lengths, filters, q_pre, rim, d_out, gathered.reshape(2, LENGTH, WIDTH)
    )
    part = part.reshape((2, 2) + SIZES + (ROWS, WIDTH))
    d_q, d_k, d_v, d_filters = scatter(doc_lengths, filters, part, dq, taps)
    return d_q, d_k, d_v, d_filters[:9].reshape(3, 3, WIDTH)


def solution(mesh):
    split = P(None, "ctx", "tp")
    return jax.shard_map(
        shards,
        mesh=mesh,
        in_specs=(split, split, split, split, P(), P()),
        out_specs=(split, split, split, P()),
        check_vma=False,
    )
```

time: 1240 us -> 140 us (0.11)
  waiting for transfers between devices: 929 us -> 0 us
  Pallas kernels: 0 us -> 125 us
  matrix products: 121 us -> 0 us
  blocking collectives: 78.9 us -> 0 us
  other arithmetic: 51.5 us -> 0 us
  local copies, waits for them, and re-layouts: 30.2 us -> 11.6 us
  starting transfers between devices: 13.9 us -> 0 us
  between operations: 14.1 us -> 0.68 us
    all_gather x2 -> x0, waiting for transfers between devices: 600 us -> none  [the longest x1 300 us: shards(): lax.all_gather(v_conv, 'ctx', axis=1, tiled=True)]
    reduce_scatter x1 -> x0, waiting for transfers between devices: 325 us -> none  [shards(): lax.psum_scatter(key_value_grads, 'ctx', scatter_dimension=1, tiled=True)]
    pallas_call x0 -> x3, Pallas kernels: none -> 125 us  [the longest x1 46.8 us: scatter(): pl.pallas_call(scatter_kernel, out_shape=(jax.ShapeDtypeStruct((2, ROWS,...]
    dot_general x112 -> x0, matrix products: 121 us -> none  [the longest x32 43.7 us: products(): jnp.einsum('qkgd,nkd->kgqn', grad_flat[row_lower:], values_part, preferre...]
    psum x1 -> x0, blocking collectives: 78.9 us -> none  [shards(): d_filters = lax.psum(local_filters, ('ctx', 'tp'))]
    dynamic_update_slice x16 -> x0, other arithmetic: 31.3 us -> none  [grads_tile(): lax.dynamic_update_slice(key_value_grads, current + joined, (part_index,...]
    ppermute x4 -> x0, starting transfers between devices: 13.8 us -> none  [the longest x2 9.26 us: padded(): lax.ppermute(lax.slice_in_dim(block, 0, width, axis=dim), axis, backward)]
  transfers between devices with their start and end apart: 7 -> 0, of which waited for: 4 -> 0; matrix products, arithmetic and copies ran while one was open for 1% -> 0% of each run, Pallas kernels for 0% -> 0%
where the time goes in v1:
time: 140 us; the launch traced here: 138 us
  Pallas kernels  125 us (89%)
  local copies, waits for them, and re-layouts  11.6 us (8%)
    pallas_call x1, Pallas kernels, scatter(): pl.pallas_call(scatter_kernel, out_shape=(jax.ShapeDtypeStruct((2, ROWS,...  46.8 us
    pallas_call x1, Pallas kernels, gather(): pl.pallas_call(gather_kernel, out_shape=(jax.ShapeDtypeStruct((2, 2) + SI...  46.8 us
    pallas_call x1, Pallas kernels, attend(): pl.pallas_call(attend_kernel, out_shape=(jax.ShapeDtypeStruct((2, ROWS, H...  31.8 us
    unnamed x23, local copies, waits for them, and re-layouts  11 us

profile of v1, /device:TPU:32, one launch (start us, length us, event | category | flops | bytes accessed | tf_op | source)
XLA Modules:
  0.0 137.6 jit_solution(12755207152872903991)
XLA Ops:
  0.6 0.0 copy-start.2
  0.6 0.9 copy-done.2
  1.6 0.0 copy-start.5
  1.6 0.8 copy-done.5
  2.3 0.0 copy-start.6
  2.3 0.8 copy-done.6
  3.1 0.0 copy-start.9
  3.1 46.8 %gather.1 = (bf16[2,2,2,4,8,64,128]{6,5,4,3,2,1,0:T(8,128)(2,1)S(1)}, bf16[2,16,1024]{2,1,0:T(8,128)(2,1)S(1)}) custom-call(bf16[2,64,128]{2,1,0:T(8,128)(2,1)S(1)} %copy-done.5, bf16[2,64,128]{2,1,0:T(8,128)(2,1)S(1)} %copy-done.6, bf16[2,64,1024]{2,1,0:T(8,128)(2,1)S(1)} %copy-done.2), custom_call_target="tpu_custom_call" | custom-call | tf_op jit(solution)/shard_map/gather/pallas_call | solution.py:159
  49.9 0.0 copy-start.1
  49.9 1.9 %copy-done.1 = bf16[2,2,2,4,8,64,128]{6,5,4,3,2,1,0:T(8,128)(2,1)} copy-done((bf16[2,2,2,4,8,64,128]{6,5,4,3,2,1,0:T(8,128)(2,1)}, bf16[2,2,2,4,8,64,128]{6,5,4,3,2,1,0:T(8,128)(2,1)S(1)}, u32[]{:S(2)}) %copy-start.1) | copy-done | bytes 4194328
  51.8 0.0 copy-start.4
  51.8 0.6 copy-done.4
  52.5 31.8 %attend.1 = (f32[2,64,1024]{2,1,0:T(8,128)}, bf16[2,8192,128]{2,1,0:T(8,128)(2,1)}, f32[16,128]{1,0:T(8,128)}) custom-call(s32[8]{0:T(128)} %lengths_ref.3, f32[3,3,128]{2,1,0:T(4,128)} %filters_ref.3, bf16[2,64,1024]{2,1,0:T(8,128)(2,1)} %q_ref.3, bf16[2,16,1024]{2,1,0:T(8,128)(2,1)} %copy-done.4, bf16[2,64,1024]{2,1,0:T(8,128)(2,1)} %do_ref.1, ...), custom_call_target="tpu_custom_call" | custom-call | tf_op jit(solution)/shard_map/attend/pallas_call | solution.py:382
  84.3 0.0 copy-done.7
  84.3 0.0 copy-done.9
  84.3 0.0 copy-start
  84.3 2.2 %copy-done = bf16[2,8192,128]{2,1,0:T(8,128)(2,1)S(1)} copy-done((bf16[2,8192,128]{2,1,0:T(8,128)(2,1)S(1)}, bf16[2,8192,128]{2,1,0:T(8,128)(2,1)}, u32[]{:S(2)}) %copy-start) | copy-done | bytes 4194328
  86.5 1.0 copy-done.3
  87.5 0.7 copy-done.8
  88.2 46.8 %scatter.1 = (f32[2,64,1024]{2,1,0:T(8,128)S(1)}, f32[2,64,128]{2,1,0:T(8,128)S(1)}, f32[2,64,128]{2,1,0:T(8,128)S(1)}, f32[16,128]{1,0:T(8,128)S(1)}) custom-call(s32[8]{0:T(128)S(1)} %copy-done.9, f32[3,3,128]{2,1,0:T(4,128)S(1)} %copy-done.7, bf16[2,2,2,4,8,64,128]{6,5,4,3,2,1,0:T(8,128)(2,1)S(1)} %bitcast.3, f32[2,64,1024]{2,1,0:T(8,128)S(1)} %copy-done.3, ...), custom_call_target="tpu_custom_call" | custom-call | tf_op jit(solution)/shard_map/scatter/pallas_call | solution.py:632
  135.0 0.6 reshape.19
  135.6 0.8 copy.13
  136.4 0.6 copy.14
  137.0 0.6 copy.15
  (3 shorter events, 0.0 us)
Async XLA Ops:
  0.6 1.0 copy-start.2
  1.6 0.8 copy-start.5
  2.3 0.8 copy-start.6
  3.1 81.2 %copy-start.7 = (f32[3,3,128]{2,1,0:T(4,128)S(1)}, f32[3,3,128]{2,1,0:T(4,128)}, u32[]{:S(2)}) copy-start(f32[3,3,128]{2,1,0:T(4,128)} %filters_ref.3) | copy-start | bytes 13828
  3.1 81.2 %copy-start.9 = (s32[8]{0:T(128)S(1)}, s32[8]{0:T(128)}, u32[]{:S(2)}) copy-start(s32[8]{0:T(128)} %lengths_ref.3) | copy-start | bytes 100
  49.9 2.0 %copy-start.1 = (bf16[2,2,2,4,8,64,128]{6,5,4,3,2,1,0:T(8,128)(2,1)}, bf16[2,2,2,4,8,64,128]{6,5,4,3,2,1,0:T(8,128)(2,1)S(1)}, u32[]{:S(2)}) copy-start(bf16[2,2,2,4,8,64,128]{6,5,4,3,2,1,0:T(8,128)(2,1)S(1)} %get-tuple-element.14) | copy-start | bytes 12582916
  51.8 0.6 copy-start.4
  84.3 2.2 %copy-start = (bf16[2,8192,128]{2,1,0:T(8,128)(2,1)S(1)}, bf16[2,8192,128]{2,1,0:T(8,128)(2,1)}, u32[]{:S(2)}) copy-start(bf16[2,8192,128]{2,1,0:T(8,128)(2,1)} %get-tuple-element.15) | copy-start | bytes 12582916
  86.5 1.0 copy-start.3
  87.5 0.7 copy-start.8

commit v2 on v1

v2 whole, which is shorter than its diff:
```python
import math

import jax
import jax.numpy as jnp
from jax import lax
from jax.experimental import pallas as pl
from jax.experimental.pallas import tpu as pltpu
from jax.sharding import PartitionSpec as P

MESH = pl.DeviceIdType.MESH
Y, X, Z = 0, 1, 2
SIZES = (2, 4, 8)
CTX = 64
TP = 4
ROWS = 64
LENGTH = 8192
HEADS = 8
WIDTH = 128
COLS = HEADS * ROWS
TILE = 512
N_TILES = LENGTH // TILE
MAX_TILES = (2 * (TILE - 1) + LENGTH // 2 + ROWS - 1) // TILE
SCALE = WIDTH ** (-0.5)
LOG2E = math.log2(math.e)
F32 = jnp.float32
BF16 = jnp.bfloat16

GATHER_PLAN = (
    (0, 0, 0, 64, (Y, X, Z), ("pair", "all4", "ring8")),
    (1, 1, 0, 64, (Y, Z, X), ("pair", "two8", "ring4")),
    (0, 1, 0, 64, (X, Z, Y), ("all4", "ring8", "pair")),
    (1, 0, 0, 64, (Z, X, Y), ("all8", "ring4", "pair")),
)
SCATTER_PLAN = (
    (0, 0, 0, 64, (Y, X, Z), ("pair", "ring4", "ring8")),
    (1, 1, 0, 64, (Y, X, Z), ("pair", "ring4", "ring8")),
    (0, 1, 0, 64, (Z, X, Y), ("ring8", "ring4", "pair")),
    (1, 0, 0, 64, (Z, Y, X), ("ring8", "pair", "ring4")),
)

WAYS = {
    "pair": ((1, 0, None, None),),
    "ring4": ((1, 0, None, None), (-1, 0, None, None), (1, -1, 0, 0), (-1, 1, 1, 1)),
    "all4": ((2, 0, None, None), (1, 0, None, None), (-1, 0, None, None)),
    "ring8": (
        (1, 0, None, None), (-1, 0, None, None), (1, -1, None, 0), (-1, 1, None, 1),
        (1, -2, None, 2), (-1, 2, None, 3), (1, -3, 0, 4), (-1, 3, 1, 5),
    ),
    "three8": (
        (2, 0, None, None), (-2, 0, None, None), (1, 0, None, None), (-1, 0, None, None),
        (1, -2, None, 0), (-1, 2, None, 1), (1, -3, 0, 4), (-1, 3, 1, 5),
    ),
    "two8": (
        (2, 0, None, None), (-2, 0, None, None), (1, 0, None, None), (-1, 0, None, None),
        (2, -2, 0, 0), (-2, 2, 1, 1), (1, -2, None, 0), (-1, 2, None, 1),
    ),
    "all8": (
        (4, 0, None, None), (3, 0, None, None), (-3, 0, None, None), (2, 0, None, None), (-2, 0, None, None),
        (1, 0, None, None), (-1, 0, None, None),
    ),
}

LINK, LATENCY, FURTHER, ISSUE, ADD = 54e3, 2.1, 0.6, 0.06, 0.0003
ROW_BYTES = WIDTH * 2


def displacements(steps):
    found = {(s.link[0], far % SIZES[s.link[0]]) for s in steps if s.link for far in (s.link[1], -s.link[1])}
    return sorted(found)


def count_of(dims):
    return math.prod(SIZES[d] for d in dims)


class Step:
    def __init__(self, chunk, after=(), needs=(), link=None, blocks=0.0, adds=0.0, **what):
        self.chunk, self.after, self.needs, self.link = chunk, list(after), list(needs), link
        self.blocks, self.adds = blocks, adds
        self.__dict__.update(what)


def gather_steps(plan):
    steps = []

    def add(*args, **what):
        steps.append(Step(*args, **what))
        return len(steps) - 1

    for chunk, (_, _, _, rows, order, ways) in enumerate(plan):
        by_stage = []
        for stage, dim in enumerate(order):
            region = {d: None if s < stage else 0 for s, d in enumerate(order)}
            bundle = rows * count_of(order[:stage])
            here = []
            if stage == 2 and SIZES[dim] == 2:
                axis = order[1]
                region[axis] = 0
                here.append(
                    add(chunk, by_stage[0], link=(dim, 1), blocks=bundle / SIZES[axis], region=region, part=None)
                )
                for i in by_stage[1]:
                    there = dict(region)
                    there[axis] = steps[i].region[axis] - steps[i].link[1]
                    here.append(
                        add(chunk, [i], link=(dim, 1), blocks=steps[i].blocks, region=there, part=steps[i].part)
                    )
            else:
                for far, offset, part, first in WAYS[ways[stage]]:
                    there = dict(region)
                    there[dim] = offset
                    after = [here[first]] if first is not None else by_stage[-1] if stage else []
                    here.append(
                        add(
                            chunk, after, link=(dim, far), blocks=bundle * (1 if part is None else 0.5),
                            region=there, part=part,
                        )
                    )
            by_stage.append(here)
    return steps


def scatter_steps(plan):
    steps = []

    def add(*args, **what):
        steps.append(Step(*args, **what))
        return len(steps) - 1

    for chunk, (_, _, _, rows, order, ways) in enumerate(plan):
        ready = None
        for stage in range(3):
            dim = order[2 - stage]
            n = SIZES[dim]
            bundle = rows * count_of(order[: 2 - stage])
            if stage == 0 and n == 2:
                axis = order[1]
                m = SIZES[axis]
                ready = {}
                offsets = [m // 2] + [sign * o for o in range(m // 2 - 1, 0, -1) for sign in (1, -1)] + [0]
                for piece, offset in enumerate(offsets):
                    what = dict(stage=0, piece=piece, offset=offset)
                    i = add(chunk, link=(dim, 1), blocks=bundle / m, kind="piece", **what)
                    ready[offset % m] = add(chunk, [i], adds=bundle / m, kind="close_piece", **what)
                continue

            def own(offset):
                return [] if ready is None else [ready[offset % n if len(ready) > 1 else 0]]

            way = WAYS[ways[2 - stage]]
            made = {}
            for e in reversed(range(len(way))):
                far, offset, part, _ = way[e]
                inner = [k for k in range(len(way)) if way[k][3] == e]
                made[e] = add(
                    chunk, [made[k] for k in inner], own(offset - far), link=(dim, -far),
                    blocks=bundle * (1 if part is None else 0.5), adds=bundle if stage or inner else 0,
                    kind="send", stage=stage, entry=e, inner=inner, offset=offset - far, part=part,
                )
            outer = [k for k in range(len(way)) if way[k][3] is None]
            ready = {
                0: add(
                    chunk, [made[k] for k in outer], own(0), adds=bundle * len(outer),
                    kind="close", stage=stage, outer=outer,
                )
            }
    return steps


def in_order(steps):
    left = [len(s.after) + len(s.needs) for s in steps]
    users = [[] for _ in steps]
    for i, s in enumerate(steps):
        for j in s.after + s.needs:
            users[j].append(i)

    def wire(s):
        return abs(s.link[1]) * s.blocks * ROW_BYTES / LINK

    def late(s):
        return LATENCY + FURTHER * (abs(s.link[1]) - 1)

    rest = [0.0] * len(steps)
    for i in reversed(range(len(steps))):
        s = steps[i]
        own = ISSUE + s.adds * ADD + (wire(s) + late(s) if s.link else 0.0)
        rest[i] = own + max([rest[u] for u in users[i]], default=0.0)
    ready = [(0.0, -rest[i], i) for i in range(len(steps)) if left[i] == 0]
    when = [0.0] * len(steps)
    order, times, busy, now = [], [], {}, 0.0
    while ready:
        now = max(now, min(ready)[0])
        pick = min((r for r in ready if r[0] <= now), key=lambda r: r[1:])
        ready.remove(pick)
        i = pick[2]
        s = steps[i]
        order.append(i)
        times.append(now)
        now += ISSUE + s.adds * ADD
        seen = now
        if s.link:
            link = (s.link[0], s.link[1] > 0)
            busy[link] = max(now, busy.get(link, 0.0)) + wire(s)
            seen = busy[link] + late(s)
        for u in users[i]:
            when[u] = max(when[u], seen if i in steps[u].after else now)
            left[u] -= 1
            if left[u] == 0:
                ready.append((when[u], -rest[u], u))
    return order, times
def coords():
    c = lax.axis_index("ctx")
    return [c // 32, (c // 8) % 4, c % 8]


def ctx_of(co):
    return co[0] * 32 + co[1] * 8 + co[2]


def shifted(co, dim, by):
    co = list(co)
    co[dim] = (co[dim] + by + SIZES[dim]) % SIZES[dim]
    return co


def block_at(half, dim, at):
    return at if half == 0 else SIZES[dim] - 1 - at


def gather_kernel(k_ref, v_ref, q_ref, g_ref, rim_ref, send_sem, recv_sem, rim_send, rim_recv, own_sem):
    c = lax.axis_index("ctx")
    co = coords()
    after, before = (c + 1) % CTX, (c + CTX - 1) % CTX
    steps = gather_steps(GATHER_PLAN)
    neighbours = [ctx_of(shifted(co, *to)) for to in displacements(steps)] + [after, before]
    barrier = pltpu.get_barrier_semaphore()
    for neighbour in neighbours:
        pl.semaphore_signal(barrier, inc=1, device_id={"ctx": neighbour}, device_id_type=MESH)
    own = []
    for half in range(2):
        at = [block_at(half, d, co[d]) for d in range(3)]
        for which, source in ((0, k_ref), (1, v_ref)):
            copy = pltpu.make_async_copy(
                source.at[half], g_ref.at[which, half, at[0], at[1], at[2]], own_sem.at[which, half]
            )
            copy.start()
            own.append(copy)
    for copy in own:
        copy.wait()
    pl.semaphore_wait(barrier, len(neighbours))

    order, _ = in_order(steps)
    copies, rims, seen = {}, [], set()
    for n, i in enumerate(order):
        s = steps[i]
        for j in s.after:
            if j not in seen:
                copies[j].wait_recv()
                seen.add(j)
        which, half, row, rows, _, _ = GATHER_PLAN[s.chunk]
        at = []
        for d in range(3):
            if s.region[d] is None:
                at.append(pl.ds(0, SIZES[d]))
            else:
                at.append(block_at(half, d, shifted(co, d, s.region[d])[d]))
        if s.part is not None:
            rows = rows // 2
            row = row + s.part * rows
        ref = g_ref.at[which, half, at[0], at[1], at[2], pl.ds(row, rows)]
        copies[i] = pltpu.make_async_remote_copy(
            src_ref=ref,
            dst_ref=ref,
            send_sem=send_sem.at[i],
            recv_sem=recv_sem.at[i],
            device_id={"ctx": ctx_of(shifted(co, *s.link))},
            device_id_type=MESH,
        )
        copies[i].start()
        if n == len(order) // 4:
            for side, target in ((0, after), (1, before)):
                copy = pltpu.make_async_remote_copy(
                    src_ref=q_ref.at[side, pl.ds(ROWS - 16, 16)],
                    dst_ref=rim_ref.at[side],
                    send_sem=rim_send.at[side],
                    recv_sem=rim_recv.at[side],
                    device_id={"ctx": target},
                    device_id_type=MESH,
                )
                copy.start()
                rims.append(copy)
    for i in order:
        if i not in seen:
            copies[i].wait_recv()
    for copy in rims:
        copy.wait()
    for i in order:
        copies[i].wait_send()


def gather(k, v, q):
    count = len(gather_steps(GATHER_PLAN))
    hbm = pl.BlockSpec(memory_space=pltpu.HBM)
    return pl.pallas_call(
        gather_kernel,
        out_shape=(
            jax.ShapeDtypeStruct((2, 2) + SIZES + (ROWS, WIDTH), BF16),
            jax.ShapeDtypeStruct((2, 16, HEADS * WIDTH), BF16),
        ),
        in_specs=[hbm] * 3,
        out_specs=(hbm,) * 2,
        scratch_shapes=[
            pltpu.SemaphoreType.DMA((count,)),
            pltpu.SemaphoreType.DMA((count,)),
            pltpu.SemaphoreType.DMA((2,)),
            pltpu.SemaphoreType.DMA((2,)),
            pltpu.SemaphoreType.DMA((2, 2)),
        ],
        compiler_params=pltpu.CompilerParams(
            collective_id=1, has_side_effects=True, vmem_limit_bytes=60 << 20
        ),
        name="gather",
    )(k, v, q)


def doc_starts(lengths_ref):
    starts = [jnp.int32(0)]
    for d in range(7):
        starts.append(starts[-1] + lengths_ref[d])
    return starts


def start_of(places, starts):
    found = jnp.zeros_like(places)
    for s in starts[1:]:
        found = jnp.where(places >= s, s, found)
    return found


def attend_kernel(
    lengths_ref, filters_ref, q_hbm, rim_hbm, do_hbm, g_hbm,
    dq_ref, out_hbm, taps_ref,
    q_ref, rim_ref, do_ref, raw_ref, kc_ref, vc_ref, s_ref, dp_ref, dk_ref, dv_ref, qs_ref, dos_ref, dqt_ref,
    zero_ref, tap_ref, in_sem, tile_sem, out_sem,
):
    c = lax.axis_index("ctx")
    starts = doc_starts(lengths_ref)
    ends = (c * ROWS, (2 * CTX - 1 - c) * ROWS)
    heads, tails = [], []
    for half in range(2):
        heads.append(start_of(ends[half], starts) // TILE)
        tails.append((ends[half] + ROWS + TILE - 1) // TILE)
    spans = ((heads[0], tails[0]), (jnp.maximum(heads[1], tails[0]), tails[1]))

    def inside(tile):
        return jnp.logical_or(
            jnp.logical_and(tile >= heads[0], tile < tails[0]),
            jnp.logical_and(tile >= heads[1], tile < tails[1]),
        )

    def row_of(tile):
        return pl.multiple_of(tile * TILE, TILE)

    def over_spans(fn):
        for lo, hi in spans:
            lax.fori_loop(lo, hi, lambda tile, _: (fn(tile), 0)[1], 0)

    loads = [
        pltpu.make_async_copy(src, dst, in_sem.at[i])
        for i, (src, dst) in enumerate(((q_hbm, q_ref), (rim_hbm, rim_ref), (do_hbm, do_ref)))
    ]
    for copy in loads:
        copy.start()

    def tile_load(which, tile):
        rows = pl.ds(row_of(tile), TILE)
        return pltpu.make_async_copy(g_hbm.at[which, rows], raw_ref.at[which, rows], tile_sem.at[which, tile])

    def tile_store(which, tile, src):
        return pltpu.make_async_copy(src, out_hbm.at[which, pl.ds(row_of(tile), TILE)], out_sem.at[which, tile])

    def start_load(tile):
        for which in range(2):
            tile_load(which, tile).start()

    over_spans(start_load)
    zero_ref[...] = jnp.zeros((TILE, WIDTH), BF16)

    def over_blank(act):
        def body(tile, _):
            @pl.when(jnp.logical_not(inside(tile)))
            def _():
                for which in range(2):
                    act(tile_store(which, tile, zero_ref))

            return 0

        lax.fori_loop(0, N_TILES, body, 0)

    over_blank(lambda copy: copy.start())
    for copy in loads:
        copy.wait()

    def q_window(half, h):
        lanes = slice(h * WIDTH, (h + 1) * WIDTH)
        before = rim_ref[half, :, lanes]
        if half == 1:
            before = jnp.where(c == CTX - 1, q_ref[0, ROWS - 16 :, lanes], before)
        cat = jnp.concatenate([before.astype(F32), q_ref[half, :, lanes].astype(F32)], axis=0)
        return [cat[16 - s : 16 - s + ROWS] for s in range(3)]

    def q_masks(half):
        places = ends[half] + lax.broadcasted_iota(jnp.int32, (ROWS, WIDTH), 0)
        begin = start_of(places, starts)
        return [places - s >= begin for s in range(1, 3)]

    for half in range(2):
        masks = q_masks(half)
        for h in range(HEADS):
            x = q_window(half, h)
            y = filters_ref[0, 0:1] * x[0]
            for s in range(1, 3):
                y = y + jnp.where(masks[s - 1], filters_ref[0, s : s + 1] * x[s], 0.0)
            qs_ref[half, h * ROWS : (h + 1) * ROWS] = y.astype(BF16)
            dos_ref[half, h * ROWS : (h + 1) * ROWS] = do_ref[half, :, h * WIDTH : (h + 1) * WIDTH]

    def raw_window(which, tile):
        r0 = row_of(tile)
        before = raw_ref[which, pl.ds(pl.multiple_of(jnp.maximum(r0 - 16, 0), 16), 16)].astype(F32)
        first = jnp.logical_or(tile == heads[0], jnp.logical_and(tile == heads[1], heads[1] >= tails[0]))
        before = jnp.where(first, 0.0, before)
        cat = jnp.concatenate([before, raw_ref[which, pl.ds(r0, TILE)].astype(F32)], axis=0)
        return [cat[16 - s : 16 - s + TILE] for s in range(3)]

    def has_edge(tile):
        r0 = row_of(tile)
        found = jnp.logical_or(tile == 0, tile == N_TILES - 1)
        for s in starts[1:]:
            found = jnp.logical_or(found, jnp.logical_and(s >= r0 - 1, s <= r0 + TILE + 1))
        return found

    def both_ways(tile, fn):
        edge = has_edge(tile)

        @pl.when(edge)
        def _():
            places = row_of(tile) + lax.broadcasted_iota(jnp.int32, (TILE, WIDTH), 0)
            fn(tile, places)

        @pl.when(jnp.logical_not(edge))
        def _():
            fn(tile, None)

    def masked(mask, value):
        return value if mask is None else jnp.where(mask, value, 0.0)

    def back_masks(places):
        if places is None:
            return [None, None, None]
        begin = start_of(places, starts)
        return [None] + [places - s >= begin for s in range(1, 3)]

    def ahead_masks(places):
        if places is None:
            return [None, None, None]
        return [None] + [
            jnp.logical_and(places >= start_of(places + s, starts), places + s < LENGTH) for s in range(1, 3)
        ]

    def convolve(tile, places):
        masks = back_masks(places)
        r0 = row_of(tile)
        for which, dst in ((0, kc_ref), (1, vc_ref)):
            x = raw_window(which, tile)
            y = filters_ref[1 + which, 0:1] * x[0]
            for s in range(1, 3):
                y = y + masked(masks[s], filters_ref[1 + which, s : s + 1] * x[s])
            dst[pl.ds(r0, TILE)] = y.astype(BF16)

    def prepare(tile):
        for which in range(2):
            tile_load(which, tile).wait()
        both_ways(tile, convolve)
        r0 = row_of(tile)
        dk_ref[pl.ds(r0, TILE)] = jnp.zeros((TILE, WIDTH), F32)
        dv_ref[pl.ds(r0, TILE)] = jnp.zeros((TILE, WIDTH), F32)

    over_spans(prepare)

    NT = (((1,), (1,)), ((), ()))
    TN = (((0,), (0,)), ((), ()))
    for half in range(2):
        p0 = ends[half]
        t0, t1 = heads[half], tails[half]
        places = p0 + lax.broadcasted_iota(jnp.int32, (1, COLS), 1) % ROWS
        begin = start_of(places, starts)
        last_begin = start_of(p0 + ROWS - 1, starts)

        def stats_step(tile, carry, edge):
            m, l, w = carry
            r0 = row_of(tile)
            at = row_of(tile - t0)
            s = (
                lax.dot_general(kc_ref[pl.ds(r0, TILE)], qs_ref[half], NT, preferred_element_type=F32)
                * (SCALE * LOG2E)
            )
            if edge:
                keys = r0 + lax.broadcasted_iota(jnp.int32, (TILE, COLS), 0)
                s = jnp.where(jnp.logical_and(keys <= places, keys >= begin), s, -1e30)
            s_ref[pl.ds(at, TILE)] = s
            dp = (
                lax.dot_general(vc_ref[pl.ds(r0, TILE)], dos_ref[half], NT, preferred_element_type=F32)
                * SCALE
            )
            dp_ref[pl.ds(at, TILE)] = dp
            s = s.reshape(TILE // 8, 8, COLS)
            dp = dp.reshape(TILE // 8, 8, COLS)
            m_new = jnp.maximum(m, jnp.max(s, axis=0))
            factor = jnp.exp2(m - m_new)
            p = jnp.exp2(s - m_new[None])
            l = l * factor + jnp.sum(p, axis=0)
            w = w * factor + jnp.sum(p * dp, axis=0)
            return m_new, l, w

        carry = (jnp.full((8, COLS), -1e30, F32), jnp.zeros((8, COLS), F32), jnp.zeros((8, COLS), F32))
        e0 = jnp.minimum((last_begin + TILE - 1) // TILE, t1)
        e1 = jnp.maximum(e0, (p0 + 1) // TILE)
        for lo, hi, edge in ((t0, e0, True), (e0, e1, False), (e1, t1, True)):
            carry = lax.fori_loop(lo, hi, lambda tile, carry, edge=edge: stats_step(tile, carry, edge), carry)
        m, l, w = carry
        top = jnp.max(m, axis=0, keepdims=True)
        factor = jnp.exp2(m - top)
        total = jnp.sum(l * factor, axis=0, keepdims=True)
        lse = top + jnp.log2(total)
        mean = jnp.sum(w * factor, axis=0, keepdims=True) / total
        dqt_ref[...] = jnp.zeros((WIDTH, COLS), F32)

        def grads_step(tile, _):
            r0 = row_of(tile)
            at = row_of(tile - t0)
            p = jnp.exp2(s_ref[pl.ds(at, TILE)] - lse)
            ds = (p * (dp_ref[pl.ds(at, TILE)] - mean)).astype(BF16)
            dv_ref[pl.ds(r0, TILE)] += jnp.dot(p.astype(BF16), dos_ref[half], preferred_element_type=F32)
            dk_ref[pl.ds(r0, TILE)] += jnp.dot(ds, qs_ref[half], preferred_element_type=F32)
            dqt_ref[...] += lax.dot_general(kc_ref[pl.ds(r0, TILE)], ds, TN, preferred_element_type=F32)
            return 0

        lax.fori_loop(t0, t1, grads_step, 0)
        dq = jnp.transpose(dqt_ref[...])
        masks = q_masks(half)
        sums = [jnp.zeros((8, WIDTH), F32) for _ in range(3)]
        for h in range(HEADS):
            grad = dq[h * ROWS : (h + 1) * ROWS]
            dq_ref[half, :, h * WIDTH : (h + 1) * WIDTH] = grad
            x = q_window(half, h)
            for s in range(3):
                term = grad * x[s]
                if s:
                    term = jnp.where(masks[s - 1], term, 0.0)
                sums[s] = sums[s] + jnp.sum(term.reshape(ROWS // 8, 8, WIDTH), axis=0)
        for s in range(3):
            tap_ref[s] = sums[s] if half == 0 else tap_ref[s] + sums[s]

    tap_ref[3:9] = jnp.zeros((6, 8, WIDTH), F32)

    def finish(tile, places):
        back, ahead = back_masks(places), ahead_masks(places)
        r0 = row_of(tile)
        beyond = pl.ds(pl.multiple_of(jnp.minimum(r0 + TILE, LENGTH - 8), 8), 8)
        more = inside(tile + 1)
        for which, acc, stage in ((0, dk_ref, kc_ref), (1, dv_ref, vc_ref)):
            x = raw_window(which, tile)
            here = acc[pl.ds(r0, TILE)]
            cat = jnp.concatenate([here, jnp.where(more, acc[beyond], 0.0)], axis=0)
            y = filters_ref[1 + which, 0:1] * here
            for s in range(1, 3):
                y = y + masked(ahead[s], filters_ref[1 + which, s : s + 1] * cat[s : s + TILE])
            stage[pl.ds(r0, TILE)] = y.astype(BF16)
            for s in range(3):
                term = masked(back[s], here * x[s])
                tap_ref[3 + 3 * which + s] += jnp.sum(term.reshape(TILE // 8, 8, WIDTH), axis=0)

    def staged(which, tile):
        return (kc_ref, vc_ref)[which].at[pl.ds(row_of(tile), TILE)]

    def finish_tile(tile):
        both_ways(tile, finish)
        for which in range(2):
            tile_store(which, tile, staged(which, tile)).start()

    over_spans(finish_tile)
    taps_ref[...] = jnp.zeros((16, WIDTH), F32)
    for i in range(9):
        taps_ref[i : i + 1] = jnp.sum(tap_ref[i], axis=0, keepdims=True)

    def wait_store(tile):
        for which in range(2):
            tile_store(which, tile, staged(which, tile)).wait()

    over_spans(wait_store)
    over_blank(lambda copy: copy.wait())


def attend(lengths, filters, q, rim, d_out, gathered):
    vmem = pl.BlockSpec(memory_space=pltpu.VMEM)
    hbm = pl.BlockSpec(memory_space=pltpu.HBM)
    return pl.pallas_call(
        attend_kernel,
        out_shape=(
            jax.ShapeDtypeStruct((2, ROWS, HEADS * WIDTH), F32),
            jax.ShapeDtypeStruct((2, LENGTH, WIDTH), BF16),
            jax.ShapeDtypeStruct((16, WIDTH), F32),
        ),
        in_specs=[pl.BlockSpec(memory_space=pltpu.SMEM), vmem] + [hbm] * 4,
        out_specs=(vmem, hbm, vmem),
        scratch_shapes=[
            pltpu.VMEM((2, ROWS, HEADS * WIDTH), BF16),
            pltpu.VMEM((2, 16, HEADS * WIDTH), BF16),
            pltpu.VMEM((2, ROWS, HEADS * WIDTH), BF16),
            pltpu.VMEM((2, LENGTH, WIDTH), BF16),
            pltpu.VMEM((LENGTH, WIDTH), BF16),
            pltpu.VMEM((LENGTH, WIDTH), BF16),
            pltpu.VMEM((MAX_TILES * TILE, COLS), F32),
            pltpu.VMEM((MAX_TILES * TILE, COLS), F32),
            pltpu.VMEM((LENGTH, WIDTH), F32),
            pltpu.VMEM((LENGTH, WIDTH), F32),
            pltpu.VMEM((2, COLS, WIDTH), BF16),
            pltpu.VMEM((2, COLS, WIDTH), BF16),
            pltpu.VMEM((WIDTH, COLS), F32),
            pltpu.VMEM((TILE, WIDTH), BF16),
            pltpu.VMEM((9, 8, WIDTH), F32),
            pltpu.SemaphoreType.DMA((3,)),
            pltpu.SemaphoreType.DMA((2, N_TILES)),
            pltpu.SemaphoreType.DMA((2, N_TILES)),
        ],
        compiler_params=pltpu.CompilerParams(vmem_limit_bytes=60 << 20),
        name="attend",
    )(lengths, filters, q, rim, d_out, gathered)


def scatter_kernel(
    lengths_ref, filters_ref, part_hbm, dq_hbm, taps_hbm,
    dqp_ref, dkp_ref, dvp_ref, dfil_ref,
    *scratch,
):
    n_chunks = len(SCATTER_PLAN)
    came = scratch[: 3 * n_chunks]
    stash = scratch[3 * n_chunks : 6 * n_chunks]
    sums = scratch[6 * n_chunks : 8 * n_chunks]
    (
        part_ref, dq_ref, rim_ref, tap_in, tap_out,
        send_sem, recv_sem, rim_send, rim_recv, tap_send, tap_recv, part_sem,
    ) = scratch[8 * n_chunks :]
    c = lax.axis_index("ctx")
    tp = lax.axis_index("tp")
    co = coords()
    after, before = (c + 1) % CTX, (c + CTX - 1) % CTX
    steps = scatter_steps(SCATTER_PLAN)

    def flipped(value, bit):
        return value + bit - 2 * bit * ((value // bit) % 2)

    partners = []
    for dim, bit in ((Z, 1), (Z, 2), (Z, 4), (X, 1), (X, 2), (Y, 1)):
        place = list(co)
        place[dim] = flipped(co[dim], bit)
        partners.append((ctx_of(place), tp))
    partners += [(c, flipped(tp, 1)), (c, flipped(tp, 2))]
    near = set(displacements(steps)) | {(Z, 1), (Z, 7), (Z, 2), (Z, 6), (Z, 4), (X, 1), (X, 3), (X, 2), (Y, 1)}
    greet = [(ctx_of(shifted(co, *to)), tp) for to in sorted(near)]
    greet += [(after, tp), (before, tp)] + partners[-2:]
    barrier = pltpu.get_barrier_semaphore()
    for ctx, core in greet:
        pl.semaphore_signal(barrier, inc=1, device_id={"ctx": ctx, "tp": core}, device_id_type=MESH)
    loads = [
        pltpu.make_async_copy(part_hbm.at[which, half], part_ref.at[which, half], part_sem.at[2 * which + half])
        for which in range(2)
        for half in range(2)
    ]
    loads.append(pltpu.make_async_copy(dq_hbm, dq_ref, part_sem.at[4]))
    loads.append(pltpu.make_async_copy(taps_hbm, tap_out.at[0], part_sem.at[5]))
    for copy in loads:
        copy.start()
    pl.semaphore_wait(barrier, len(greet))

    def send(src, dst, send_at, recv_at, ctx, core):
        copy = pltpu.make_async_remote_copy(
            src_ref=src, dst_ref=dst, send_sem=send_at, recv_sem=recv_at,
            device_id={"ctx": ctx, "tp": core}, device_id_type=MESH,
        )
        copy.start()
        return copy

    loaded = set()

    def load(i):
        if i not in loaded:
            loads[i].wait()
            loaded.add(i)

    def blocks(dims, fn):
        sizes = [SIZES[d] for d in dims]

        def body(i, _):
            at = []
            for size in reversed(sizes):
                at.append(i % size)
                i = i // size
            fn(tuple(reversed(at)))
            return 0

        if sizes:
            lax.fori_loop(0, math.prod(sizes), body, 0)
        else:
            fn(())

    def own_at(s, target):
        which, half, row0, _, order, _ = SCATTER_PLAN[s.chunk]
        dim = order[2 - s.stage]
        kept = sorted(order[: 2 - s.stage])
        dims = sorted(order[: 3 - s.stage])
        if s.stage == 0:
            load(2 * which + half)

        def value(at, row, count):
            where = dict(zip(kept, at))
            where[dim] = target
            full = tuple(where[d] for d in dims)
            if s.stage == 0:
                return part_ref[(which, half, *full, pl.ds(row0 + row, count))].astype(F32)
            return sums[2 * s.chunk + s.stage - 1][(*full, pl.ds(row, count))]

        return value

    def run_send(i, s):
        which, half, row0, rows, order, ways = SCATTER_PLAN[s.chunk]
        dim = order[2 - s.stage]
        kept = sorted(order[: 2 - s.stage])
        whole = tuple(pl.ds(0, SIZES[d]) for d in kept)
        target = block_at(half, dim, shifted(co, dim, s.offset)[dim])
        arrived = came[3 * s.chunk + s.stage]
        mid = rows // 2
        row, count = (0, rows) if s.part is None else (s.part * mid, mid)
        if s.stage == 0 and not s.inner:
            where = [pl.ds(0, SIZES[d]) for d in range(3)]
            where[dim] = target
            src = part_hbm.at[(which, half, *where, pl.ds(row0 + row, count))]
        else:
            held = stash[3 * s.chunk + s.stage]
            own = own_at(s, target)
            way = WAYS[ways[2 - s.stage]]
            split = s.part is None and any(way[k][2] is not None for k in s.inner)

            def merge(at):
                for part in (0, 1) if split else (None,):
                    lo, n = (part * mid, mid) if split else (row, count)
                    value = own(at, lo, n)
                    for k in s.inner:
                        if not split or way[k][2] in (None, part):
                            value = value + arrived[(k, *at, pl.ds(lo, n))].astype(F32)
                    held[(s.entry, *at, pl.ds(lo, n))] = value.astype(BF16)

            blocks(kept, merge)
            src = held.at[(s.entry, *whole, pl.ds(row, count))]
        dst = arrived.at[(s.entry, *whole, pl.ds(row, count))]
        return send(src, dst, send_sem.at[i], recv_sem.at[i], ctx_of(shifted(co, *s.link)), tp)

    def run_close(s):
        which, half, row0, rows, order, _ = SCATTER_PLAN[s.chunk]
        dim = order[2 - s.stage]
        kept = sorted(order[: 2 - s.stage])
        own = own_at(s, block_at(half, dim, co[dim]))
        arrived = came[3 * s.chunk + s.stage]

        def total(at):
            value = own(at, 0, rows)
            for k in s.outer:
                value = value + arrived[(k, *at)].astype(F32)
            if s.stage < 2:
                sums[2 * s.chunk + s.stage][at] = value
            else:
                (dkp_ref if which == 0 else dvp_ref)[half, pl.ds(row0, rows)] = value

        blocks(kept, total)

    def run_piece(i, s):
        which, half, row0, rows, order, _ = SCATTER_PLAN[s.chunk]
        _, axis, dim = order
        where = [pl.ds(0, SIZES[d]) for d in range(3)]
        where[dim] = block_at(half, dim, shifted(co, dim, 1)[dim])
        where[axis] = block_at(half, axis, shifted(co, axis, s.offset)[axis])
        return send(
            part_hbm.at[(which, half, *where, pl.ds(row0, rows))], came[3 * s.chunk].at[s.piece],
            send_sem.at[i], recv_sem.at[i], ctx_of(shifted(co, *s.link)), tp,
        )

    def run_close_piece(s):
        which, half, row0, rows, order, _ = SCATTER_PLAN[s.chunk]
        first, axis, dim = order
        mine = block_at(half, dim, co[dim])
        target = block_at(half, axis, shifted(co, axis, s.offset)[axis])
        load(2 * which + half)

        def total(at):
            where = {first: at[0], axis: target, dim: mine}
            value = part_ref[(which, half, *(where[d] for d in range(3)), pl.ds(row0, rows))].astype(F32)
            value = value + came[3 * s.chunk][(s.piece, *at)].astype(F32)
            sums[2 * s.chunk][tuple(where[d] for d in sorted((first, axis)))] = value

        blocks([first], total)

    tap_copies = []

    def tap_start():
        k = len(tap_copies)
        tap_copies.append(send(tap_out.at[k], tap_in.at[k], tap_send.at[k], tap_recv.at[k], *partners[k]))

    def tap_sum():
        k = len(tap_copies) - 1
        tap_copies[k].wait_recv()
        return tap_out[k] + tap_in[k]

    def query_gradient():
        load(4)
        for copy in rims:
            copy.wait_recv()
        starts = doc_starts(lengths_ref)
        for half in range(2):
            p0 = c * ROWS if half == 0 else (2 * CTX - 1 - c) * ROWS
            places = p0 + lax.broadcasted_iota(jnp.int32, (ROWS, WIDTH), 0)
            ahead = [
                jnp.logical_and(places >= start_of(places + s, starts), places + s < LENGTH) for s in range(1, 3)
            ]
            for h in range(HEADS):
                lanes = slice(h * WIDTH, (h + 1) * WIDTH)
                beyond = rim_ref[half, :, lanes]
                if half == 0:
                    beyond = jnp.where(c == CTX - 1, dq_ref[1, 0:8, lanes], beyond)
                here = dq_ref[half, :, lanes]
                cat = jnp.concatenate([here, beyond], axis=0)
                y = filters_ref[0, 0:1] * here
                for s in range(1, 3):
                    y = y + jnp.where(ahead[s - 1], filters_ref[0, s : s + 1] * cat[s : s + ROWS], 0.0)
                dqp_ref[half, :, lanes] = y

    order, times = in_order(steps)
    copies, seen = {}, set()
    rims = []
    first = 0
    while steps[order[first]].link and not steps[order[first]].after and not steps[order[first]].needs:
        first += 1
    pace = (times[-1] - times[first]) / 8
    marks = {max(n for n, t in enumerate(times) if t <= times[first] + pace * k): k for k in range(1, 8)}
    for n, i in enumerate(order):
        s = steps[i]
        for j in s.after:
            if steps[j].link and j not in seen:
                copies[j].wait_recv()
                seen.add(j)
        if s.kind == "send":
            copies[i] = run_send(i, s)
        elif s.kind == "piece":
            copies[i] = run_piece(i, s)
        elif s.kind == "close":
            run_close(s)
        else:
            run_close_piece(s)
        if n + 1 == first:
            for half, target in ((0, before), (1, after)):
                rims.append(
                    send(
                        dq_hbm.at[half, pl.ds(0, 8)], rim_ref.at[half],
                        rim_send.at[half], rim_recv.at[half], target, tp,
                    )
                )
            load(5)
            tap_start()
            query_gradient()
        if n in marks:
            tap_out[marks[n]] = tap_sum()
            tap_start()
    value = tap_sum()
    for m in range(3):
        dfil_ref[m] = value[3 * m : 3 * m + 3]
    for copy in list(copies.values()) + tap_copies + rims:
        copy.wait_send()


def scatter(lengths, filters, part, dq, taps):
    vmem = pl.BlockSpec(memory_space=pltpu.VMEM)
    hbm = pl.BlockSpec(memory_space=pltpu.HBM)
    count = len(scatter_steps(SCATTER_PLAN))
    came, stash, sums = [], [], []
    for _, _, _, rows, order, ways in SCATTER_PLAN:
        for stage in range(3):
            kept = tuple(SIZES[d] for d in sorted(order[: 2 - stage]))
            if stage == 0 and order[2] == Y:
                shape = (SIZES[order[1]], SIZES[order[0]])
                spare = (1, 1)
            else:
                shape = spare = (len(WAYS[ways[2 - stage]]),) + kept
            came.append(pltpu.VMEM(shape + (rows, WIDTH), BF16))
            stash.append(pltpu.VMEM(spare + (rows, WIDTH), BF16))
            if stage < 2:
                sums.append(pltpu.VMEM(kept + (rows, WIDTH), F32))
    return pl.pallas_call(
        scatter_kernel,
        out_shape=(
            jax.ShapeDtypeStruct((2, ROWS, HEADS * WIDTH), F32),
            jax.ShapeDtypeStruct((2, ROWS, WIDTH), F32),
            jax.ShapeDtypeStruct((2, ROWS, WIDTH), F32),
            jax.ShapeDtypeStruct((3, 3, WIDTH), F32),
        ),
        in_specs=[pl.BlockSpec(memory_space=pltpu.SMEM), vmem] + [hbm] * 3,
        out_specs=(vmem,) * 4,
        scratch_shapes=came
        + stash
        + sums
        + [
            pltpu.VMEM((2, 2) + SIZES + (ROWS, WIDTH), BF16),
            pltpu.VMEM((2, ROWS, HEADS * WIDTH), F32),
            pltpu.VMEM((2, 8, HEADS * WIDTH), F32),
            pltpu.VMEM((8, 16, WIDTH), F32),
            pltpu.VMEM((8, 16, WIDTH), F32),
            pltpu.SemaphoreType.DMA((count,)),
            pltpu.SemaphoreType.DMA((count,)),
            pltpu.SemaphoreType.DMA((2,)),
            pltpu.SemaphoreType.DMA((2,)),
            pltpu.SemaphoreType.DMA((8,)),
            pltpu.SemaphoreType.DMA((8,)),
            pltpu.SemaphoreType.DMA((6,)),
        ],
        compiler_params=pltpu.CompilerParams(
            collective_id=2, has_side_effects=True, vmem_limit_bytes=60 << 20
        ),
        name="scatter",
    )(lengths, filters, part, dq, taps)


def deliver_kernel(*refs):
    count = len(refs) // 2
    for src, dst in zip(refs[:count], refs[count:]):
        dst[...] = src[...]


def deliver(*arrays):
    vmem = pl.BlockSpec(memory_space=pltpu.VMEM)
    return pl.pallas_call(
        deliver_kernel,
        out_shape=tuple(jax.ShapeDtypeStruct(a.shape, a.dtype) for a in arrays),
        in_specs=[vmem] * len(arrays),
        out_specs=(vmem,) * len(arrays),
        compiler_params=pltpu.CompilerParams(vmem_limit_bytes=60 << 20),
        name="deliver",
    )(*arrays)


def shards(q_pre, k_pre, value_before_filter, d_out, filters, doc_lengths):
    gathered, rim = gather(k_pre, value_before_filter, q_pre)
    dq, part, taps = attend(
        doc_lengths, filters, q_pre, rim, d_out, gathered.reshape(2, LENGTH, WIDTH)
    )
    part = part.reshape((2, 2) + SIZES + (ROWS, WIDTH))
    return deliver(*scatter(doc_lengths, filters, part, dq, taps))


def solution(mesh):
    split = P(None, "ctx", "tp")
    return jax.shard_map(
        shards,
        mesh=mesh,
        in_specs=(split, split, split, split, P(), P()),
        out_specs=(split, split, split, P()),
        check_vma=False,
    )
```

time: 140 us -> 108 us (0.77); the launches traced: 138 us -> 108 us
  Pallas kernels: 125 us -> 107 us
  local copies, waits for them, and re-layouts: 11.6 us -> 0 us
    pallas_call x1, Pallas kernels: 31.8 us -> 10.5 us  [attend(): pl.pallas_call(attend_kernel, out_shape=(jax.ShapeDtypeStruct((2, ROWS, H...]
    unnamed x23 -> x0, local copies, waits for them, and re-layouts: 11 us -> none
    pallas_call x1, Pallas kernels: 46.8 us -> 57.6 us  [scatter(): pl.pallas_call(scatter_kernel, out_shape=(jax.ShapeDtypeStruct((2, ROWS,...]
    pallas_call x1, Pallas kernels: 46.8 us -> 36.9 us  [gather(): pl.pallas_call(gather_kernel, out_shape=(jax.ShapeDtypeStruct((2, 2) + SI...]
    pallas_call x0 -> x1, Pallas kernels: none -> 1.93 us  [deliver(): pl.pallas_call(deliver_kernel, out_shape=tuple((jax.ShapeDtypeStruct(a.sh...]
where the time goes in v2:
time: 108 us
  Pallas kernels  107 us (99%)
    pallas_call x1, Pallas kernels, scatter(): pl.pallas_call(scatter_kernel, out_shape=(jax.ShapeDtypeStruct((2, ROWS,...  57.6 us
    pallas_call x1, Pallas kernels, gather(): pl.pallas_call(gather_kernel, out_shape=(jax.ShapeDtypeStruct((2, 2) + SI...  36.9 us
    pallas_call x1, Pallas kernels, attend(): pl.pallas_call(attend_kernel, out_shape=(jax.ShapeDtypeStruct((2, ROWS, H...  10.5 us

profile of v2, /device:TPU:32, one launch (start us, length us, event | category | flops | bytes accessed | tf_op | source)
XLA Modules:
  0.0 107.6 jit_solution(7287775364536222653)
XLA Ops:
  0.6 36.9 %gather.1 = (bf16[2,2,2,4,8,64,128]{6,5,4,3,2,1,0:T(8,128)(2,1)}, bf16[2,16,1024]{2,1,0:T(8,128)(2,1)}) custom-call(bf16[2,64,128]{2,1,0:T(8,128)(2,1)} %k_ref.1, bf16[2,64,128]{2,1,0:T(8,128)(2,1)} %v_ref.1, bf16[2,64,1024]{2,1,0:T(8,128)(2,1)} %q_hbm.1), custom_call_target="tpu_custom_call" | custom-call | tf_op jit(solution)/shard_map/gather/pallas_call | solution.py:304
  37.6 10.5 %attend.1 = (f32[2,64,1024]{2,1,0:T(8,128)}, bf16[2,8192,128]{2,1,0:T(8,128)(2,1)}, f32[16,128]{1,0:T(8,128)}) custom-call(s32[8]{0:T(128)} %lengths_ref.3, f32[3,3,128]{2,1,0:T(4,128)} %filters_ref.3, bf16[2,64,1024]{2,1,0:T(8,128)(2,1)} %q_hbm.1, bf16[2,16,1024]{2,1,0:T(8,128)(2,1)} %get-tuple-element.13.rim_hbm, bf16[2,64,1024]{2,1,0:T(8,128)(2,1)} %do_hbm.1, ...), custom_call_target="tpu_custom_call" | custom-call | tf_op jit(solution)/shard_map/attend/pallas_call | solution.py:607
  48.1 57.6 %scatter.1 = (f32[2,64,1024]{2,1,0:T(8,128)}, f32[2,64,128]{2,1,0:T(8,128)}, f32[2,64,128]{2,1,0:T(8,128)}, f32[3,3,128]{2,1,0:T(4,128)}) custom-call(s32[8]{0:T(128)} %lengths_ref.3, f32[3,3,128]{2,1,0:T(4,128)} %filters_ref.3, bf16[2,2,2,4,8,64,128]{6,5,4,3,2,1,0:T(8,128)(2,1)} %bitcast.2, f32[2,64,1024]{2,1,0:T(8,128)} %get-tuple-element.16.dq_hbm, ...), custom_call_target="tpu_custom_call" | custom-call | tf_op jit(solution)/shard_map/scatter/pallas_call | solution.py:906
  105.7 1.9 %deliver.1 = (f32[2,64,1024]{2,1,0:T(8,128)}, f32[2,64,128]{2,1,0:T(8,128)}, f32[2,64,128]{2,1,0:T(8,128)}, f32[3,3,128]{2,1,0:T(4,128)}) custom-call(f32[2,64,1024]{2,1,0:T(8,128)} %get-tuple-element.18.refs_0_, f32[2,64,128]{2,1,0:T(8,128)} %get-tuple-element.19.refs_1_, f32[2,64,128]{2,1,0:T(8,128)} %get-tuple-element.20.refs_2_, ...), custom_call_target="tpu_custom_call" | custom-call | tf_op jit(solution)/shard_map/deliver/pallas_call | solution.py:948

commit v3 on v2

--- a/solution.py
+++ b/solution.py
@@ -26,17 +26,16 @@
 BF16 = jnp.bfloat16
 
 GATHER_PLAN = (
-    (0, 0, 0, 64, (Y, X, Z), ("pair", "all4", "ring8")),
-    (1, 1, 0, 64, (Y, Z, X), ("pair", "two8", "ring4")),
-    (0, 1, 0, 64, (X, Z, Y), ("all4", "ring8", "pair")),
-    (1, 0, 0, 64, (Z, X, Y), ("all8", "ring4", "pair")),
+    (0, 0, 0, 32, (Y, X, Z), ("pair", "all4", "ring8")),
+    (1, 1, 0, 32, (Y, X, Z), ("pair", "all4", "ring8")),
+    (0, 1, 0, 32, (Y, X, Z), ("pair", "ring4", "ring8")),
+    (1, 0, 0, 32, (X, Z, Y), ("all4", "three8", "pair")),
+    (0, 0, 32, 32, (Z, Y, X), ("two8", "pair", "ring4")),
+    (1, 1, 32, 32, (Z, Y, X), ("two8", "pair", "ring4")),
+    (0, 1, 32, 32, (Z, Y, X), ("two8", "pair", "ring4")),
+    (1, 0, 32, 32, (Z, X, Y), ("two8", "ring4", "pair")),
 )
-SCATTER_PLAN = (
-    (0, 0, 0, 64, (Y, X, Z), ("pair", "ring4", "ring8")),
-    (1, 1, 0, 64, (Y, X, Z), ("pair", "ring4", "ring8")),
-    (0, 1, 0, 64, (Z, X, Y), ("ring8", "ring4", "pair")),
-    (1, 0, 0, 64, (Z, Y, X), ("ring8", "pair", "ring4")),
-)
+SCATTER_PLAN = GATHER_PLAN
 
 WAYS = {
     "pair": ((1, 0, None, None),),
@@ -62,6 +61,7 @@
 
 LINK, LATENCY, FURTHER, ISSUE, ADD = 54e3, 2.1, 0.6, 0.06, 0.0003
 ROW_BYTES = WIDTH * 2
+LAG = 32
 
 
 def displacements(steps):
@@ -245,12 +245,10 @@
             )
             copy.start()
             own.append(copy)
-    for copy in own:
-        copy.wait()
     pl.semaphore_wait(barrier, len(neighbours))
 
     order, _ = in_order(steps)
-    copies, rims, seen = {}, [], set()
+    copies, rims, seen, waiting = {}, [], set(), []
     for n, i in enumerate(order):
         s = steps[i]
         for j in s.after:
@@ -268,8 +266,14 @@
             rows = rows // 2
             row = row + s.part * rows
         ref = g_ref.at[which, half, at[0], at[1], at[2], pl.ds(row, rows)]
+        if all(offset == 0 for offset in s.region.values()):
+            src = (k_ref, v_ref)[which].at[half, pl.ds(row, rows)]
+        else:
+            src = ref
+            while own:
+                own.pop().wait()
         copies[i] = pltpu.make_async_remote_copy(
-            src_ref=ref,
+            src_ref=src,
             dst_ref=ref,
             send_sem=send_sem.at[i],
             recv_sem=recv_sem.at[i],
@@ -277,6 +281,9 @@
             device_id_type=MESH,
         )
         copies[i].start()
+        waiting.append(copies[i])
+        if len(waiting) > LAG:
+            waiting.pop(0).wait_send()
         if n == len(order) // 4:
             for side, target in ((0, after), (1, before)):
                 copy = pltpu.make_async_remote_copy(
@@ -294,8 +301,8 @@
             copies[i].wait_recv()
     for copy in rims:
         copy.wait()
-    for i in order:
-        copies[i].wait_send()
+    for copy in waiting:
+        copy.wait_send()
 
 
 def gather(k, v, q):
@@ -648,7 +655,7 @@
     stash = scratch[3 * n_chunks : 6 * n_chunks]
     sums = scratch[6 * n_chunks : 8 * n_chunks]
     (
-        part_ref, dq_ref, rim_ref, tap_in, tap_out,
+        part_ref, dq_ref, rim_ref, tap_ref,
         send_sem, recv_sem, rim_send, rim_recv, tap_send, tap_recv, part_sem,
     ) = scratch[8 * n_chunks :]
     c = lax.axis_index("ctx")
@@ -657,18 +664,12 @@
     after, before = (c + 1) % CTX, (c + CTX - 1) % CTX
     steps = scatter_steps(SCATTER_PLAN)
 
-    def flipped(value, bit):
-        return value + bit - 2 * bit * ((value // bit) % 2)
-
-    partners = []
-    for dim, bit in ((Z, 1), (Z, 2), (Z, 4), (X, 1), (X, 2), (Y, 1)):
-        place = list(co)
-        place[dim] = flipped(co[dim], bit)
-        partners.append((ctx_of(place), tp))
-    partners += [(c, flipped(tp, 1)), (c, flipped(tp, 2))]
-    near = set(displacements(steps)) | {(Z, 1), (Z, 7), (Z, 2), (Z, 6), (Z, 4), (X, 1), (X, 3), (X, 2), (Y, 1)}
+    groups = [[(ctx_of(shifted(co, dim, by)), tp) for by in range(1, SIZES[dim])] for dim in (Z, X, Y)]
+    groups.insert(2, [(c, (tp + by) % TP) for by in range(1, TP)])
+    slots = (co[Z], co[X], tp, co[Y])
+    near = set(displacements(steps)) | {(dim, by) for dim in (Z, X, Y) for by in range(1, SIZES[dim])}
     greet = [(ctx_of(shifted(co, *to)), tp) for to in sorted(near)]
-    greet += [(after, tp), (before, tp)] + partners[-2:]
+    greet += [(after, tp), (before, tp)] + groups[2]
     barrier = pltpu.get_barrier_semaphore()
     for ctx, core in greet:
         pl.semaphore_signal(barrier, inc=1, device_id={"ctx": ctx, "tp": core}, device_id_type=MESH)
@@ -678,7 +679,7 @@
         for half in range(2)
     ]
     loads.append(pltpu.make_async_copy(dq_hbm, dq_ref, part_sem.at[4]))
-    loads.append(pltpu.make_async_copy(taps_hbm, tap_out.at[0], part_sem.at[5]))
+    loads.append(pltpu.make_async_copy(taps_hbm, tap_ref.at[0, slots[0]], part_sem.at[5]))
     for copy in loads:
         copy.start()
     pl.semaphore_wait(barrier, len(greet))
@@ -811,14 +812,27 @@
 
     tap_copies = []
 
-    def tap_start():
+    def tap_start(value):
         k = len(tap_copies)
-        tap_copies.append(send(tap_out.at[k], tap_in.at[k], tap_send.at[k], tap_recv.at[k], *partners[k]))
+        mine = tap_ref.at[k, slots[k]]
+        if value is not None:
+            mine[...] = value
+        first = sum(len(group) for group in groups[:k])
+        tap_copies.append(
+            [
+                send(mine, mine, tap_send.at[first + i], tap_recv.at[first + i], *peer)
+                for i, peer in enumerate(groups[k])
+            ]
+        )
 
     def tap_sum():
         k = len(tap_copies) - 1
-        tap_copies[k].wait_recv()
-        return tap_out[k] + tap_in[k]
+        for copy in tap_copies[k]:
+            copy.wait_recv()
+        value = tap_ref[k, 0]
+        for i in range(1, len(groups[k]) + 1):
+            value = value + tap_ref[k, i]
+        return value
 
     def query_gradient():
         load(4)
@@ -844,23 +858,27 @@
                 dqp_ref[half, :, lanes] = y
 
     order, times = in_order(steps)
-    copies, seen = {}, set()
+    copies, seen, waiting = {}, set(), []
     rims = []
     first = 0
     while steps[order[first]].link and not steps[order[first]].after and not steps[order[first]].needs:
         first += 1
-    pace = (times[-1] - times[first]) / 8
-    marks = {max(n for n, t in enumerate(times) if t <= times[first] + pace * k): k for k in range(1, 8)}
+    pace = (times[-1] - times[first]) / 4
+    marks = {max(n for n, t in enumerate(times) if t <= times[first] + pace * k): k for k in range(1, 4)}
     for n, i in enumerate(order):
         s = steps[i]
+        if len(waiting) > LAG:
+            waiting.pop(0).wait_send()
         for j in s.after:
             if steps[j].link and j not in seen:
                 copies[j].wait_recv()
                 seen.add(j)
         if s.kind == "send":
             copies[i] = run_send(i, s)
+            waiting.append(copies[i])
         elif s.kind == "piece":
             copies[i] = run_piece(i, s)
+            waiting.append(copies[i])
         elif s.kind == "close":
             run_close(s)
         else:
@@ -874,15 +892,14 @@
                     )
                 )
             load(5)
-            tap_start()
+            tap_start(None)
             query_gradient()
         if n in marks:
-            tap_out[marks[n]] = tap_sum()
-            tap_start()
+            tap_start(tap_sum())
     value = tap_sum()
     for m in range(3):
         dfil_ref[m] = value[3 * m : 3 * m + 3]
-    for copy in list(copies.values()) + tap_copies + rims:
+    for copy in waiting + sum(tap_copies, []) + rims:
         copy.wait_send()
 
 
@@ -920,14 +937,13 @@
             pltpu.VMEM((2, 2) + SIZES + (ROWS, WIDTH), BF16),
             pltpu.VMEM((2, ROWS, HEADS * WIDTH), F32),
             pltpu.VMEM((2, 8, HEADS * WIDTH), F32),
-            pltpu.VMEM((8, 16, WIDTH), F32),
-            pltpu.VMEM((8, 16, WIDTH), F32),
+            pltpu.VMEM((4, 8, 16, WIDTH), F32),
             pltpu.SemaphoreType.DMA((count,)),
             pltpu.SemaphoreType.DMA((count,)),
             pltpu.SemaphoreType.DMA((2,)),
             pltpu.SemaphoreType.DMA((2,)),
-            pltpu.SemaphoreType.DMA((8,)),
-            pltpu.SemaphoreType.DMA((8,)),
+            pltpu.SemaphoreType.DMA((14,)),
+            pltpu.SemaphoreType.DMA((14,)),
             pltpu.SemaphoreType.DMA((6,)),
         ],
         compiler_params=pltpu.CompilerParams(

time: 108 us -> 109 us (level)
  no operation moved by 1% of the time
where the time goes in v3:
time: 109 us; the launch traced here: 108 us
  Pallas kernels  107 us (98%)
    pallas_call x1, Pallas kernels, scatter(): pl.pallas_call(scatter_kernel, out_shape=(jax.ShapeDtypeStruct((2, ROWS,...  57.2 us
    pallas_call x1, Pallas kernels, gather(): pl.pallas_call(gather_kernel, out_shape=(jax.ShapeDtypeStruct((2, 2) + SI...  37.6 us
    pallas_call x1, Pallas kernels, attend(): pl.pallas_call(attend_kernel, out_shape=(jax.ShapeDtypeStruct((2, ROWS, H...  10.5 us

profile of v3, /device:TPU:32, one launch (start us, length us, event | category | flops | bytes accessed | tf_op | source)
XLA Modules:
  0.0 107.9 jit_solution(15052266391989660368)
XLA Ops:
  0.6 37.6 %gather.1 = (bf16[2,2,2,4,8,64,128]{6,5,4,3,2,1,0:T(8,128)(2,1)}, bf16[2,16,1024]{2,1,0:T(8,128)(2,1)}) custom-call(bf16[2,64,128]{2,1,0:T(8,128)(2,1)} %k_ref.1, bf16[2,64,128]{2,1,0:T(8,128)(2,1)} %v_ref.1, bf16[2,64,1024]{2,1,0:T(8,128)(2,1)} %q_hbm.1), custom_call_target="tpu_custom_call" | custom-call | tf_op jit(solution)/shard_map/gather/pallas_call | solution.py:311
  38.2 10.5 %attend.1 = (f32[2,64,1024]{2,1,0:T(8,128)}, bf16[2,8192,128]{2,1,0:T(8,128)(2,1)}, f32[16,128]{1,0:T(8,128)}) custom-call(s32[8]{0:T(128)} %lengths_ref.3, f32[3,3,128]{2,1,0:T(4,128)} %filters_ref.3, bf16[2,64,1024]{2,1,0:T(8,128)(2,1)} %q_hbm.1, bf16[2,16,1024]{2,1,0:T(8,128)(2,1)} %get-tuple-element.13.rim_hbm, bf16[2,64,1024]{2,1,0:T(8,128)(2,1)} %do_hbm.1, ...), custom_call_target="tpu_custom_call" | custom-call | tf_op jit(solution)/shard_map/attend/pallas_call | solution.py:614
  48.7 57.2 %scatter.1 = (f32[2,64,1024]{2,1,0:T(8,128)}, f32[2,64,128]{2,1,0:T(8,128)}, f32[2,64,128]{2,1,0:T(8,128)}, f32[3,3,128]{2,1,0:T(4,128)}) custom-call(s32[8]{0:T(128)} %lengths_ref.3, f32[3,3,128]{2,1,0:T(4,128)} %filters_ref.3, bf16[2,2,2,4,8,64,128]{6,5,4,3,2,1,0:T(8,128)(2,1)} %bitcast.2, f32[2,64,1024]{2,1,0:T(8,128)} %get-tuple-element.16.dq_hbm, ...), custom_call_target="tpu_custom_call" | custom-call | tf_op jit(solution)/shard_map/scatter/pallas_call | solution.py:923
  105.9 1.9 %deliver.1 = (f32[2,64,1024]{2,1,0:T(8,128)}, f32[2,64,128]{2,1,0:T(8,128)}, f32[2,64,128]{2,1,0:T(8,128)}, f32[3,3,128]{2,1,0:T(4,128)}) custom-call(f32[2,64,1024]{2,1,0:T(8,128)} %get-tuple-element.18.refs_0_, f32[2,64,128]{2,1,0:T(8,128)} %get-tuple-element.19.refs_1_, f32[2,64,128]{2,1,0:T(8,128)} %get-tuple-element.20.refs_2_, ...), custom_call_target="tpu_custom_call" | custom-call | tf_op jit(solution)/shard_map/deliver/pallas_call | solution.py:964

commit v4 on v3

--- a/solution.py
+++ b/solution.py
@@ -59,7 +59,7 @@
     ),
 }
 
-LINK, LATENCY, FURTHER, ISSUE, ADD = 54e3, 2.1, 0.6, 0.06, 0.0003
+LINK, LATENCY, FURTHER, ISSUE, ADD = 65e3, 2.5, 0.6, 0.1, 0.0003
 ROW_BYTES = WIDTH * 2
 LAG = 32
 
@@ -346,9 +346,9 @@
 
 def attend_kernel(
     lengths_ref, filters_ref, q_hbm, rim_hbm, do_hbm, g_hbm,
-    dq_ref, out_hbm, taps_ref,
+    dq_hbm, out_hbm, taps_ref,
     q_ref, rim_ref, do_ref, raw_ref, kc_ref, vc_ref, s_ref, dp_ref, dk_ref, dv_ref, qs_ref, dos_ref, dqt_ref,
-    zero_ref, tap_ref, in_sem, tile_sem, out_sem,
+    zero_ref, tap_ref, dq_ref, in_sem, tile_sem, out_sem, dq_sem,
 ):
     c = lax.axis_index("ctx")
     starts = doc_starts(lengths_ref)
@@ -496,6 +496,7 @@
 
     NT = (((1,), (1,)), ((), ()))
     TN = (((0,), (0,)), ((), ()))
+    dq_stores = []
     for half in range(2):
         p0 = ends[half]
         t0, t1 = heads[half], tails[half]
@@ -567,6 +568,8 @@
                 sums[s] = sums[s] + jnp.sum(term.reshape(ROWS // 8, 8, WIDTH), axis=0)
         for s in range(3):
             tap_ref[s] = sums[s] if half == 0 else tap_ref[s] + sums[s]
+        dq_stores.append(pltpu.make_async_copy(dq_ref.at[half], dq_hbm.at[half], dq_sem.at[half]))
+        dq_stores[-1].start()
 
     tap_ref[3:9] = jnp.zeros((6, 8, WIDTH), F32)
 
@@ -604,6 +607,8 @@
         for which in range(2):
             tile_store(which, tile, staged(which, tile)).wait()
 
+    for copy in dq_stores:
+        copy.wait()
     over_spans(wait_store)
     over_blank(lambda copy: copy.wait())
 
@@ -619,7 +624,7 @@
             jax.ShapeDtypeStruct((16, WIDTH), F32),
         ),
         in_specs=[pl.BlockSpec(memory_space=pltpu.SMEM), vmem] + [hbm] * 4,
-        out_specs=(vmem, hbm, vmem),
+        out_specs=(hbm, hbm, vmem),
         scratch_shapes=[
             pltpu.VMEM((2, ROWS, HEADS * WIDTH), BF16),
             pltpu.VMEM((2, 16, HEADS * WIDTH), BF16),
@@ -636,9 +641,11 @@
             pltpu.VMEM((WIDTH, COLS), F32),
             pltpu.VMEM((TILE, WIDTH), BF16),
             pltpu.VMEM((9, 8, WIDTH), F32),
+            pltpu.VMEM((2, ROWS, HEADS * WIDTH), F32),
             pltpu.SemaphoreType.DMA((3,)),
             pltpu.SemaphoreType.DMA((2, N_TILES)),
             pltpu.SemaphoreType.DMA((2, N_TILES)),
+            pltpu.SemaphoreType.DMA((2,)),
         ],
         compiler_params=pltpu.CompilerParams(vmem_limit_bytes=60 << 20),
         name="attend",
@@ -647,7 +654,7 @@
 
 def scatter_kernel(
     lengths_ref, filters_ref, part_hbm, dq_hbm, taps_hbm,
-    dqp_ref, dkp_ref, dvp_ref, dfil_ref,
+    dqp_hbm, dkp_ref, dvp_ref, dfil_ref,
     *scratch,
 ):
     n_chunks = len(SCATTER_PLAN)
@@ -655,7 +662,7 @@
     stash = scratch[3 * n_chunks : 6 * n_chunks]
     sums = scratch[6 * n_chunks : 8 * n_chunks]
     (
-        part_ref, dq_ref, rim_ref, tap_ref,
+        part_ref, dq_ref, dqp_ref, rim_ref, tap_ref,
         send_sem, recv_sem, rim_send, rim_recv, tap_send, tap_recv, part_sem,
     ) = scratch[8 * n_chunks :]
     c = lax.axis_index("ctx")
@@ -856,9 +863,11 @@
                 for s in range(1, 3):
                     y = y + jnp.where(ahead[s - 1], filters_ref[0, s : s + 1] * cat[s : s + ROWS], 0.0)
                 dqp_ref[half, :, lanes] = y
+        dqp_store.start()
 
     order, times = in_order(steps)
     copies, seen, waiting = {}, set(), []
+    dqp_store = pltpu.make_async_copy(dqp_ref, dqp_hbm, part_sem.at[6])
     rims = []
     first = 0
     while steps[order[first]].link and not steps[order[first]].after and not steps[order[first]].needs:
@@ -901,6 +910,7 @@
         dfil_ref[m] = value[3 * m : 3 * m + 3]
     for copy in waiting + sum(tap_copies, []) + rims:
         copy.wait_send()
+    dqp_store.wait()
 
 
 def scatter(lengths, filters, part, dq, taps):
@@ -929,12 +939,13 @@
             jax.ShapeDtypeStruct((3, 3, WIDTH), F32),
         ),
         in_specs=[pl.BlockSpec(memory_space=pltpu.SMEM), vmem] + [hbm] * 3,
-        out_specs=(vmem,) * 4,
+        out_specs=(hbm, vmem, vmem, vmem),
         scratch_shapes=came
         + stash
         + sums
         + [
             pltpu.VMEM((2, 2) + SIZES + (ROWS, WIDTH), BF16),
+            pltpu.VMEM((2, ROWS, HEADS * WIDTH), F32),
             pltpu.VMEM((2, ROWS, HEADS * WIDTH), F32),
             pltpu.VMEM((2, 8, HEADS * WIDTH), F32),
             pltpu.VMEM((4, 8, 16, WIDTH), F32),
@@ -944,7 +955,7 @@
             pltpu.SemaphoreType.DMA((2,)),
             pltpu.SemaphoreType.DMA((14,)),
             pltpu.SemaphoreType.DMA((14,)),
-            pltpu.SemaphoreType.DMA((6,)),
+            pltpu.SemaphoreType.DMA((7,)),
         ],
         compiler_params=pltpu.CompilerParams(
             collective_id=2, has_side_effects=True, vmem_limit_bytes=60 << 20

time: 109 us -> 105 us (0.963); the launches traced: 108 us -> 105 us
  Pallas kernels: 107 us -> 105 us
    pallas_call x1, Pallas kernels: 57.2 us -> 54.9 us  [scatter(): pl.pallas_call(scatter_kernel, out_shape=(jax.ShapeDtypeStruct((2, ROWS,...]
where the time goes in v4:
time: 105 us
  Pallas kernels  105 us (100%)
    pallas_call x1, Pallas kernels, scatter(): pl.pallas_call(scatter_kernel, out_shape=(jax.ShapeDtypeStruct((2, ROWS,...  54.9 us
    pallas_call x1, Pallas kernels, gather(): pl.pallas_call(gather_kernel, out_shape=(jax.ShapeDtypeStruct((2, 2) + SI...  37.5 us
    pallas_call x1, Pallas kernels, attend(): pl.pallas_call(attend_kernel, out_shape=(jax.ShapeDtypeStruct((2, ROWS, H...  10.3 us

profile of v4, /device:TPU:32, one launch (start us, length us, event | category | flops | bytes accessed | tf_op | source)
XLA Modules:
  0.0 105.3 jit_solution(13049660443980854599)
XLA Ops:
  0.6 37.5 %gather.1 = (bf16[2,2,2,4,8,64,128]{6,5,4,3,2,1,0:T(8,128)(2,1)}, bf16[2,16,1024]{2,1,0:T(8,128)(2,1)}) custom-call(bf16[2,64,128]{2,1,0:T(8,128)(2,1)} %k_ref.1, bf16[2,64,128]{2,1,0:T(8,128)(2,1)} %v_ref.1, bf16[2,64,1024]{2,1,0:T(8,128)(2,1)} %q_hbm.1), custom_call_target="tpu_custom_call" | custom-call | tf_op jit(solution)/shard_map/gather/pallas_call | solution.py:311
  38.1 10.3 %attend.1 = (f32[2,64,1024]{2,1,0:T(8,128)}, bf16[2,8192,128]{2,1,0:T(8,128)(2,1)}, f32[16,128]{1,0:T(8,128)}) custom-call(s32[8]{0:T(128)} %lengths_ref.3, f32[3,3,128]{2,1,0:T(4,128)} %filters_ref.3, bf16[2,64,1024]{2,1,0:T(8,128)(2,1)} %q_hbm.1, bf16[2,16,1024]{2,1,0:T(8,128)(2,1)} %get-tuple-element.13.rim_hbm, bf16[2,64,1024]{2,1,0:T(8,128)(2,1)} %do_hbm.1, ...), custom_call_target="tpu_custom_call" | custom-call | tf_op jit(solution)/shard_map/attend/pallas_call | solution.py:619
  48.4 54.9 %scatter.1 = (f32[2,64,1024]{2,1,0:T(8,128)}, f32[2,64,128]{2,1,0:T(8,128)}, f32[2,64,128]{2,1,0:T(8,128)}, f32[3,3,128]{2,1,0:T(4,128)}) custom-call(s32[8]{0:T(128)} %lengths_ref.3, f32[3,3,128]{2,1,0:T(4,128)} %filters_ref.3, bf16[2,2,2,4,8,64,128]{6,5,4,3,2,1,0:T(8,128)(2,1)} %bitcast.2, f32[2,64,1024]{2,1,0:T(8,128)} %get-tuple-element.16.dq_hbm, ...), custom_call_target="tpu_custom_call" | custom-call | tf_op jit(solution)/shard_map/scatter/pallas_call | solution.py:933
  103.3 1.9 %deliver.1 = (f32[2,64,1024]{2,1,0:T(8,128)}, f32[2,64,128]{2,1,0:T(8,128)}, f32[2,64,128]{2,1,0:T(8,128)}, f32[3,3,128]{2,1,0:T(4,128)}) custom-call(f32[2,64,1024]{2,1,0:T(8,128)} %get-tuple-element.18.refs_0_, f32[2,64,128]{2,1,0:T(8,128)} %get-tuple-element.19.refs_1_, f32[2,64,128]{2,1,0:T(8,128)} %get-tuple-element.20.refs_2_, ...), custom_call_target="tpu_custom_call" | custom-call | tf_op jit(solution)/shard_map/deliver/pallas_call | solution.py:975
